TPU v7x, 256 devices: a whole 4x4x8 slice. The times are simulated.
256 devices in a mesh: island: 64 (over z, y, core), shard: 4 (over x).
Axes of the slice: x: 4, y: 4, z: 8, core: 2. Of those that a mesh axis runs over, the one named last changes fastest.
Arguments:
- weight: bfloat16 [256, 8192], P('shard'), may hold values from -0.0625 to 0.0625
- acts_t: bfloat16 [256, 16384], P('shard', 'island')
- out_grad: bfloat16 [16384, 8192], P('island')
- momentum: bfloat16 [64, 256, 8192], P('island', 'shard'), may hold values from -6 to 6
- chosen: int32 [64, 64], P('island', 'shard'), may hold values from 0 to 16383, as said below
- counts: int32 [64, 4], P('island', 'shard'), may hold values from 1 to 16, as said below
- steps: int32 [64], P('island'), may hold values from 1 to 32
Outputs:
- update: bfloat16 [256, 8192], P('shard')
- momentum_next: bfloat16 [64, 256, 8192], P('island', 'shard')
- acts_grad: bfloat16 [256, 16384], P('shard', 'island')
Inputs may be any that keep to these rules, and one draw needn't show every extreme that they name: `chosen`: row i holds, for each shard s at places s * 16 to (s + 1) * 16 - 1, distinct block numbers from s * 4096 to (s + 1) * 4096 - 1; only the first counts[i, s] of them are selected. `counts`: some device's count is 16.
All inputs are finite; a program needn't handle non-finite values.
Results may differ from a plain program's by a relative error of at most 0.001.
Values sent between devices are 32-bit elements; how exact they have to be, the bound alone decides.
No kernel may reach another device: no remote copies, remote signals or barrier semaphores. Data moves between devices by JAX's collectives and lax.ppermute only.
A program may use at most 128 MiB of HBM per device.

v0:
```python
import math

import jax
import jax.numpy as jnp
from jax import lax
from jax.sharding import PartitionSpec as P


def cosine_table():
    freq = jnp.arange(64, dtype=jnp.float32)[:, None]
    place = jnp.arange(64, dtype=jnp.float32)[None, :]
    waves = jnp.cos(jnp.pi * (2.0 * place + 1.0) * freq / 128.0)
    return jnp.where(freq == 0.0, 0.125, math.sqrt(2.0 / 64.0)) * waves


def paired(cosine):
    zeroes = jnp.zeros_like(cosine)
    upper = jnp.concatenate([cosine, zeroes], 1)
    lower = jnp.concatenate([zeroes, cosine], 1)
    return jnp.concatenate([upper, lower], 0)


def apply_tiles(matrix, left_side, right_side):
    row_count, column_count = matrix.shape
    strips = matrix.reshape(row_count // 64, 64, column_count)
    blended = jnp.einsum("ij,ajn->ain", left_side, strips, precision=lax.Precision.HIGHEST)
    lanewise = blended.reshape(row_count, column_count // 128, 128)
    result = jnp.dot(lanewise, right_side, precision=lax.Precision.HIGHEST)
    return result.reshape(row_count, column_count)


def to_blocks(matrix):
    row_count, column_count = matrix.shape
    shaped = matrix.reshape(row_count // 8, 8, column_count // 16, 16)
    return shaped.transpose(0, 2, 1, 3).reshape(-1, 128)


def from_blocks(blocks, row_count, column_count):
    shaped = blocks.reshape(row_count // 8, column_count // 16, 8, 16)
    return shaped.transpose(0, 2, 1, 3).reshape(row_count, column_count)


def clip_factor(grad_weight, entry_count):
    squares = lax.psum(jnp.sum(grad_weight * grad_weight), "shard")
    return jnp.minimum(1.0, 1.0 / jnp.sqrt(squares / entry_count + 1e-06))


def on_device(weight, acts_t, out_grad, momentum, chosen, counts, steps):
    row_count, column_count = weight.shape
    islands = lax.axis_size("island")
    shards = lax.axis_size("shard")
    cosine = cosine_table()
    forward_right = paired(cosine.T)
    inverse_right = paired(cosine)
    grad_weight = jnp.dot(acts_t, out_grad, preferred_element_type=jnp.float32)
    acts_grad = lax.dot_general(
        weight, out_grad, (((1,), (1,)), ((), ())), preferred_element_type=jnp.float32
    ).astype(jnp.bfloat16)
    entry_count = float(row_count * column_count * shards)
    momentum_in = momentum[0].astype(jnp.float32)
    factor = clip_factor(grad_weight, entry_count)
    combined = 0.9 * momentum_in + factor * grad_weight
    blocks = to_blocks(apply_tiles(combined, cosine, forward_right))
    block_count = blocks.shape[0]
    slot_count = chosen.shape[1]
    own_blocks = chosen[0] - lax.axis_index("shard") * block_count
    live_slots = jnp.arange(slot_count, dtype=jnp.int32) < counts[0, 0]
    matches = (
        jnp.arange(block_count, dtype=jnp.int32)[:, None] == own_blocks[None, :]
    ) & live_slots[None, :]
    picked = jnp.any(matches, axis=1).astype(jnp.float32)
    remaining = blocks * (1.0 - picked)[:, None]
    momentum_next = apply_tiles(
        from_blocks(remaining, row_count, column_count), cosine.T, inverse_right
    ).astype(jnp.bfloat16)[None]
    island_steps = steps[0].astype(jnp.float32)
    dense_grid = blocks * (picked * island_steps)[:, None]
    summed, total_steps = lax.psum((dense_grid, island_steps), "island")
    merged = summed * (islands / total_steps)
    update = apply_tiles(
        from_blocks(merged, row_count, column_count), cosine.T, inverse_right
    ).astype(jnp.bfloat16)
    return (update, momentum_next, acts_grad)


def solution(mesh):
    placed = (
        P("shard", None),
        P("shard", "island"),
        P("island", None),
        P("island", "shard", None),
        P("island", "shard"),
        P("island", "shard"),
        P("island"),
    )
    return jax.shard_map(
        on_device,
        mesh=mesh,
        in_specs=placed,
        out_specs=(P("shard", None), P("island", "shard", None), P("shard", "island")),
        check_vma=False,
    )
```

profile of v0, /device:TPU:1, one launch (start us, length us, event | category | flops | bytes accessed | tf_op | source)
XLA Modules:
  0.0 287.4 jit_solution(14714972520922195838)
XLA Ops:
  7.2 0.0 copy-start
  7.2 0.0 all-reduce.6.cloned.1.call-start
  8.6 3.7 %multiply_reduce_fusion = (f32[]{:T(128)}, f32[64,8192]{1,0:T(8,128)S(1)}) fusion(bf16[64,256]{1,0:T(8,128)(2,1)} %param.8, bf16[256,8192]{1,0:T(8,128)(2,1)} %param.9), kind=kOutput, calls=%fused_computation.6 | convolution fusion | flops 269484032 | bytes 6324228 | tf_op jit(solution)/shard_map/dot_general | solution.py:55
  12.3 9.9 %psum.21 = f32[]{:T(128)} all-reduce(f32[]{:T(128)} %get-tuple-element.7), channel_id=1, replica_groups=mesh['island'=64,'shard'=4] {'shard'}, use_global_device_ids=true, to_apply=%region_1.2 | all-reduce | flops 1 | bytes 8 | tf_op jit(solution)/shard_map/psum | solution.py:44
  22.9 0.3 cosine_multiply_fusion.1
  23.2 3.7 %fusion.6 = f32[8,8,64,128]{3,1,2,0:T(8,128)S(1)} fusion(f32[64,8192]{1,0:T(8,128)S(1)} %get-tuple-element.8, bf16[1,64,8192]{2,1,0:T(8,128)(2,1)} %param.10, f32[]{:T(128)S(6)} %min.3, f32[64]{0:T(128)S(1)} %get-tuple-element.10, f32[64]{0:T(128)S(1)} %get-tuple-element.9), kind=kOutput, calls=%fused_computation.9 | convolution fusion | flops 404762624 | bytes 5243396 | tf_op jit(solution)/shard_map/ij,ajn->ain/dot_general | solution.py:26
  26.9 0.4 copy.14
  27.3 1.8 fusion.14
  29.1 8.4 %reshape_reshape.7 = f32[8,8,512,16]{3,2,1,0:T(8,128)} reshape(f32[64,64,128]{2,1,0:T(8,128)S(1)} %fusion.14) | data formatting | bytes 4194304 | tf_op jit(solution)/shard_map/reshape;reshape | solution.py:34
  37.6 11.0 %copy.12 = f32[8,512,8,16]{1,0,3,2:T(8,128)} copy(f32[8,512,8,16]{3,1,2,0:T(8,128)} %bitcast.73) | data formatting | bytes 4194304 | tf_op jit(solution)/shard_map/transpose | solution.py:35
  48.6 4.6 %copy.15 = f32[16,8,8,512]{3,1,2,0:T(8,128)} copy(f32[16,8,8,512]{3,2,1,0:T(8,128)} %bitcast.75) | data formatting | bytes 4194304
  53.2 0.1 fusion.11
  53.3 3.2 %broadcast_multiply_fusion.1 = f32[4096,128]{0,1:T(8,128)} fusion(f32[4096,128]{0,1:T(8,128)} %bitcast.77, f32[4096]{0:T(1024)S(1)} %get-tuple-element.4), kind=kLoop, calls=%fused_computation.17 | loop fusion | flops 524288 | bytes 4210688 | tf_op jit(solution)/shard_map/mul | solution.py:77
  56.5 0.0 all-reduce.6.cloned.1.call-update
  56.5 130.7 %psum.23 = f32[]{:T(128)} all-reduce(f32[]{:T(128)} %bitcast.7), channel_id=1, replica_groups=mesh['island'=64,'shard'=4] {'island'}, use_global_device_ids=true, to_apply=%region_4.5 | all-reduce | flops 1 | bytes 8 | tf_op jit(solution)/shard_map/psum | solution.py:78
  187.2 7.8 %mul.210 = f32[8,8,512,16]{3,2,1,0:T(8,128)} broadcast(f32[8,512]{1,0:T(8,128)S(1)} %sub.24), dimensions={0,2} | broadcast | bytes 2113536 | tf_op jit(solution)/shard_map/mul | solution.py:72
  195.0 15.3 %mul.211 = f32[64,8192]{1,0:T(8,128)} reshape(f32[8,8,512,16]{3,2,1,0:T(8,128)} %mul.210) | data formatting | bytes 4194304 | tf_op jit(solution)/shard_map/mul | solution.py:72
  210.4 5.0 %fusion.7 = f32[8,8,64,128]{3,1,2,0:T(8,128)S(1)} fusion(f32[64,8192]{1,0:T(8,128)} %mul.211, f32[8,8,64,128]{3,2,1,0:T(8,128)S(1)} %bitcast.74, f32[64]{0:T(128)S(1)} %get-tuple-element.10, f32[64]{0:T(128)S(1)} %get-tuple-element.9), kind=kOutput, calls=%fused_computation.10 | convolution fusion | flops 403189760 | bytes 6291968 | tf_op jit(solution)/shard_map/ij,ajn->ain/dot_general | solution.py:26
  215.4 0.4 copy.20
  215.7 1.8 convolution_convert_fusion
  217.6 1.3 convert_element_type.47
  219.6 0.0 copy-done
  219.6 4.2 %convolution_convert_fusion.2 = bf16[64,256]{1,0:T(8,128)(2,1)} fusion(bf16[64,8192]{1,0:T(8,128)(2,1)S(1)} %copy-done, bf16[256,8192]{1,0:T(8,128)(2,1)} %param.9), kind=kOutput, calls=%fused_computation.14 | convolution fusion | flops 268451840 | bytes 5275648 | tf_op jit(solution)/shard_map/dot_general | solution.py:56
  223.8 24.6 %all-reduce.6.cloned.1.call-done = f32[4096,128]{0,1:T(8,128)} async-done(((f32[4096,128]{0,1:T(8,128)}), f32[4096,128]{0,1:T(8,128)}) %all-reduce.6.cloned.1.call-update) | async-done | bytes 2097168 | tf_op jit(solution)/shard_map/psum | solution.py:78
  248.4 1.8 broadcast_multiply_fusion
  250.2 1.6 copy.16
  251.8 8.6 %copy.13 = f32[8,8,512,16]{3,2,1,0:T(8,128)} copy(f32[8,8,512,16]{2,0,3,1:T(8,128)S(1)} %bitcast.76) | data formatting | bytes 4194304 | tf_op jit(solution)/shard_map/transpose | solution.py:40
  260.4 14.2 %reshape.93 = f32[64,8192]{1,0:T(8,128)S(1)} reshape(f32[8,8,512,16]{3,2,1,0:T(8,128)} %copy.13) | data formatting | bytes 4194304 | tf_op jit(solution)/shard_map/reshape.2
  274.6 2.0 convolution_bitcast_fusion
  276.6 0.4 copy.17
  277.0 1.8 convolution_convert_fusion.1
  278.9 1.7 copy.28
  (7 shorter events, 0.0 us)
Async XLA Ops:
  7.2 212.4 %copy-start = (bf16[64,8192]{1,0:T(8,128)(2,1)S(1)}, bf16[64,8192]{1,0:T(8,128)(2,1)}, u32[]{:S(2)}) copy-start(bf16[64,8192]{1,0:T(8,128)(2,1)} %param.7) | copy-start | bytes 3145732
  7.2 241.3 %all-reduce.6.cloned.1.call-start = ((), (), s32[]{:S(2)}) async-start(), calls=%async_computation | async-start | bytes 4194304 | tf_op jit(solution)/shard_map/psum | solution.py:78
  48.6 4.6 %copy-start.1 = (s32[1,16]{1,0:T(1,128)S(1)}, s32[1,16]{1,0:T(1,128)}, u32[]{:S(2)}) copy-start(s32[1,16]{1,0:T(1,128)} %param.11) | copy-start | bytes 196
Sparse Core Ops, SparseCore 0:
  56.6 191.7 all-reduce.5
where the time goes:
time: 289 us; the launch traced here: 287 us
  blocking collectives  141 us (49%)
  local copies, waits for them, and re-layouts  75.7 us (26%)
  waiting for transfers between devices  24.7 us (9%)
  matrix products  24.1 us (8%)
  between operations  16.9 us (6%)
  other arithmetic  5.39 us (2%)
    psum x1, blocking collectives, on_device(): summed, total_steps = lax.psum((dense_grid, island_steps), 'island')  131 us
    psum x1, waiting for transfers between devices, on_device(): summed, total_steps = lax.psum((dense_grid, island_steps), 'island')  24.6 us
    mul x2, local copies, waits for them, and re-layouts, on_device(): remaining = blocks * (1.0 - picked)[:, None]  23.1 us
    another operation x1, local copies, waits for them, and re-layouts  14.2 us
    transpose x1, local copies, waits for them, and re-layouts, to_blocks(): return shaped.transpose(0, 2, 1, 3).reshape(-1, 128)  11 us
    dot_general x3, matrix products, apply_tiles(): jnp.einsum('ij,ajn->ain', left_side, strips, precision=lax.Precision.HIGH...  10.7 us
    psum x1, blocking collectives, clip_factor(): squares = lax.psum(jnp.sum(grad_weight * grad_weight), 'shard')  9.9 us
    unnamed x10, local copies, waits for them, and re-layouts  9.06 us
  transfers between devices with their start and end apart: 1, of which 1 were waited for; matrix products, arithmetic and copies ran while one was open for 12% of the time, Pallas kernels for 0%

commit v1 on v0

v1 whole, which is shorter than its diff:
```python
import functools

import jax
import jax.numpy as jnp
import ml_dtypes
import numpy as np
from jax import lax
from jax.experimental import pallas as pl
from jax.experimental.pallas import tpu as pltpu
from jax.sharding import PartitionSpec as P

BF = jnp.bfloat16
F32 = jnp.float32
SLOTS = 16
PAY = SLOTS * 128
MIB = 1 << 20


def dct_matrix():
    freq = np.arange(64, dtype=np.float64)[:, None]
    place = np.arange(64, dtype=np.float64)[None, :]
    waves = np.cos(np.pi * (2.0 * place + 1.0) * freq / 128.0)
    return np.where(freq == 0.0, 0.125, np.sqrt(2.0 / 64.0)) * waves


def halves(a):
    hi = a.astype(ml_dtypes.bfloat16)
    lo = (a - hi.astype(np.float64)).astype(ml_dtypes.bfloat16)
    return hi, lo


COS = dct_matrix()
COS_HI, COS_LO = halves(COS)
INV_HI, INV_LO = halves(COS.T)


def diagonal(a, copies):
    return np.kron(np.eye(copies), a.astype(np.float64)).astype(ml_dtypes.bfloat16)


FWD_LEFT3 = np.concatenate([COS_HI, COS_HI, COS_LO], 1)
FWD_LEFT2 = np.concatenate([COS_HI, COS_LO], 1)
INV_LEFT3 = np.concatenate([INV_HI, INV_HI, INV_LO], 1)
FWD_RIGHT3 = np.concatenate([diagonal(COS_HI.T, 2), diagonal(COS_HI.T, 2), diagonal(COS_LO.T, 2)], 0)
INV_RIGHT3 = np.concatenate([diagonal(COS_HI, 2), diagonal(COS_HI, 2), diagonal(COS_LO, 2)], 0)
INV_WIDE_HI = diagonal(COS_HI, 4)
INV_WIDE_LO = diagonal(COS_LO, 4)


def split(x):
    hi = x.astype(BF)
    return hi, (x - hi.astype(F32)).astype(BF)


def dot(a, b):
    return jnp.dot(a, b, preferred_element_type=F32)


def grad_kernel(acts, og, grad, squares, total):
    step = pl.program_id(0)

    @pl.when(step == 0)
    def _():
        total[...] = jnp.zeros_like(total)

    g = dot(acts[...], og[...])
    grad[...] = g
    rows, width = g.shape
    total[...] += jnp.sum((g * g).reshape(rows // 8, 8, width), axis=0)

    @pl.when(step == pl.num_programs(0) - 1)
    def _():
        squares[...] = jnp.full(squares.shape, jnp.sum(total[...]), F32)


def grad_call(acts, og, chunk=1024):
    rows, toks = acts.shape
    cols = og.shape[1]
    return pl.pallas_call(
        grad_kernel,
        grid=(cols // chunk,),
        in_specs=[
            pl.BlockSpec((rows, toks), lambda i: (0, 0)),
            pl.BlockSpec((toks, chunk), lambda i: (0, i)),
        ],
        out_specs=[
            pl.BlockSpec((rows, chunk), lambda i: (0, i)),
            pl.BlockSpec((1, 128), lambda i: (0, 0)),
        ],
        out_shape=[
            jax.ShapeDtypeStruct((rows, cols), F32),
            jax.ShapeDtypeStruct((1, 128), F32),
        ],
        scratch_shapes=[pltpu.VMEM((8, chunk), F32)],
        compiler_params=pltpu.CompilerParams(vmem_limit_bytes=24 * MIB),
        cost_estimate=pl.CostEstimate(flops=2 * rows * toks * cols, bytes_accessed=6 * MIB, transcendentals=0),
        name="weight_grad",
    )(acts, og)


def acts_grad_kernel(weight, og, out, total):
    step = pl.program_id(0)

    @pl.when(step == 0)
    def _():
        total[...] = jnp.zeros_like(total)

    total[...] += lax.dot_general(
        weight[...], og[...], (((1,), (1,)), ((), ())), preferred_element_type=F32
    )

    @pl.when(step == pl.num_programs(0) - 1)
    def _():
        out[...] = total[...].astype(BF)


def acts_grad_call(weight, og, chunk=1024):
    rows, cols = weight.shape
    toks = og.shape[0]
    return pl.pallas_call(
        acts_grad_kernel,
        grid=(cols // chunk,),
        in_specs=[
            pl.BlockSpec((rows, chunk), lambda i: (0, i)),
            pl.BlockSpec((toks, chunk), lambda i: (0, i)),
        ],
        out_specs=pl.BlockSpec((rows, toks), lambda i: (0, 0)),
        out_shape=jax.ShapeDtypeStruct((rows, toks), BF),
        scratch_shapes=[pltpu.VMEM((rows, toks), F32)],
        compiler_params=pltpu.CompilerParams(vmem_limit_bytes=24 * MIB),
        cost_estimate=pl.CostEstimate(flops=2 * rows * toks * cols, bytes_accessed=5 * MIB, transcendentals=0),
        name="acts_grad",
    )(weight, og)


def lane_group(shape):
    return lax.broadcasted_iota(jnp.int32, shape, 1) >> 4


def coef_kernel(picks, counts, momentum, grad, left2, left3, right3,
                coef_m, coef_g, pack_m, pack_g,
                mom_in, grad_in, side_m, side_g, low, sem):
    def copies(j):
        pair = (picks[j] >> 3) & 63
        cols = pl.ds(pl.multiple_of(pair * 128, 128), 128)
        here = pl.ds(j * 128, 128)
        return (
            pltpu.make_async_copy(momentum.at[:, cols], mom_in.at[:, here], sem.at[0, j]),
            pltpu.make_async_copy(grad.at[:, cols], grad_in.at[:, here], sem.at[1, j]),
        )

    for j in range(SLOTS):
        for c in copies(j):
            c.start()
    for j in range(SLOTS):
        for c in copies(j):
            c.wait()
    m = mom_in[...]
    g_hi, g_lo = split(grad_in[...])
    side_m[...] = dot(left2[...], jnp.concatenate([m, m], 0))
    side_g[...] = dot(left3[...], jnp.concatenate([g_hi, g_lo, g_hi], 0))
    for j in range(SLOTS):
        rows = pl.ds(pl.multiple_of((picks[j] >> 9) * 8, 8), 8)
        low[8 * j:8 * j + 8, :] = side_m[rows, 128 * j:128 * j + 128]
        low[128 + 8 * j:136 + 8 * j, :] = side_g[rows, 128 * j:128 * j + 128]
    hi, lo = split(low[...])
    low[...] = dot(jnp.concatenate([hi, lo, hi], 1), right3[...])
    group = lane_group((8, 128))
    live = counts[0]
    for base, coef, pack in ((0, coef_m, pack_m), (128, coef_g, pack_g)):
        packed = [jnp.zeros((8, 128), F32)] * 2
        for j in range(SLOTS):
            off = picks[j] & 7
            want = jnp.where(j < live, off, 8)
            kept = jnp.where(group == want, low[base + 8 * j:base + 8 * j + 8, :], 0.0)
            coef[8 * j:8 * j + 8, :] = kept
            turned = pltpu.roll(kept, ((j % 8 - off) & 7) * 16, 1)
            packed[j // 8] = packed[j // 8] + turned
        pack[0:8, :] = packed[0]
        pack[8:16, :] = packed[1]


def coef_call(picks, counts, momentum, grad):
    rows, cols = grad.shape
    vm = pl.BlockSpec(memory_space=pltpu.VMEM)
    sm = pl.BlockSpec(memory_space=pltpu.SMEM)
    anyw = pl.BlockSpec(memory_space=pl.ANY)
    return pl.pallas_call(
        coef_kernel,
        in_specs=[sm, sm, anyw, anyw, vm, vm, vm],
        out_specs=[vm] * 4,
        out_shape=[
            jax.ShapeDtypeStruct((128, 128), F32),
            jax.ShapeDtypeStruct((128, 128), F32),
            jax.ShapeDtypeStruct((16, 128), F32),
            jax.ShapeDtypeStruct((16, 128), F32),
        ],
        scratch_shapes=[
            pltpu.VMEM((rows, PAY), BF),
            pltpu.VMEM((rows, PAY), F32),
            pltpu.VMEM((rows, PAY), F32),
            pltpu.VMEM((rows, PAY), F32),
            pltpu.VMEM((256, 128), F32),
            pltpu.SemaphoreType.DMA((2, SLOTS)),
        ],
        compiler_params=pltpu.CompilerParams(vmem_limit_bytes=24 * MIB),
        cost_estimate=pl.CostEstimate(flops=200_000_000, bytes_accessed=3 * MIB, transcendentals=0),
        name="selected_coefs",
    )(picks, counts, momentum, grad, FWD_LEFT2, FWD_LEFT3, FWD_RIGHT3)


def rest_kernel(picks, factor, coef_m, coef_g, momentum, grad, left3, right3, out, full, wide):
    f = factor[0]
    wide[...] = jnp.zeros_like(wide)
    hi, lo = split(0.9 * coef_m[...] + f * coef_g[...])
    low = dot(jnp.concatenate([hi, lo, hi], 1), right3[...])
    for j in range(SLOTS):
        rows = pl.ds(pl.multiple_of((picks[j] >> 9) * 8, 8), 8)
        wide[rows, 128 * j:128 * j + 128] = low[8 * j:8 * j + 8, :]
    hi, lo = split(wide[...])
    wide[...] = dot(left3[...], jnp.concatenate([hi, lo, hi], 0))
    cols = full.shape[1]
    for c in range(0, cols, 1024):
        at = slice(c, c + 1024)
        full[:, at] = 0.9 * momentum[:, at].astype(F32) + f * grad[:, at]
    for j in range(SLOTS):
        pair = (picks[j] >> 3) & 63
        at = pl.ds(pl.multiple_of(pair * 128, 128), 128)
        full[:, at] = full[:, at] - wide[:, 128 * j:128 * j + 128]
    for c in range(0, cols, 1024):
        at = slice(c, c + 1024)
        out[:, at] = full[:, at].astype(BF)


def rest_call(picks, factor, coef_m, coef_g, momentum, grad):
    rows, cols = grad.shape
    vm = pl.BlockSpec(memory_space=pltpu.VMEM)
    sm = pl.BlockSpec(memory_space=pltpu.SMEM)
    return pl.pallas_call(
        rest_kernel,
        in_specs=[sm, sm] + [vm] * 6,
        out_specs=vm,
        out_shape=jax.ShapeDtypeStruct((rows, cols), BF),
        scratch_shapes=[pltpu.VMEM((rows, cols), F32), pltpu.VMEM((rows, PAY), F32)],
        compiler_params=pltpu.CompilerParams(vmem_limit_bytes=24 * MIB),
        cost_estimate=pl.CostEstimate(flops=100_000_000, bytes_accessed=4 * MIB, transcendentals=0),
        name="momentum_rest",
    )(picks, factor, coef_m, coef_g, momentum, grad, INV_LEFT3, INV_RIGHT3)


def merge_kernel(picks, scale, own, other, left3, wide_hi, wide_lo, out, grid, side):
    grid[...] = jnp.zeros_like(grid)
    group = lane_group((8, 128))
    islands = own.shape[0]

    def add_islands(pay, first):
        def one(i, carry):
            tiles = [pay[i, 0:8, :], pay[i, 8:16, :]]
            base = (first + i) * SLOTS
            olds, news, masks, places = [], [], [], []
            for j in range(SLOTS):
                b = picks[base + j]
                off = b & 7
                place = b >> 3
                turned = pltpu.roll(tiles[j // 8], ((off - j % 8) & 7) * 16, 1)
                olds.append(grid[place])
                news.append(turned)
                masks.append(group == off)
                places.append(place)
            for j in range(SLOTS):
                pltpu.store(grid.at[places[j]], olds[j] + news[j], mask=masks[j])
            return carry

        lax.fori_loop(0, islands, one, 0)

    add_islands(own, 0)
    add_islands(other, islands)
    s = scale[0]
    pairs = grid.shape[0] // 8

    def left(c, carry):
        parts = []
        for k in range(2):
            parts.append(jnp.concatenate([grid[r * pairs + 2 * c + k] for r in range(8)], 0))
        hi, lo = split(jnp.concatenate(parts, 1))
        z = dot(left3[...], jnp.concatenate([hi, lo, hi], 0)) * s
        hi, lo = split(z)
        y = dot(hi, wide_hi[...]) + (dot(lo, wide_hi[...]) + dot(hi, wide_lo[...]))
        out[:, pl.ds(pl.multiple_of(c * 256, 256), 256)] = y.astype(BF)
        return carry

    lax.fori_loop(0, pairs // 2, left, 0, unroll=4)


def merge_call(picks, scale, own, other, rows, cols):
    vm = pl.BlockSpec(memory_space=pltpu.VMEM)
    sm = pl.BlockSpec(memory_space=pltpu.SMEM)
    return pl.pallas_call(
        merge_kernel,
        in_specs=[sm, sm] + [vm] * 5,
        out_specs=vm,
        out_shape=jax.ShapeDtypeStruct((rows, cols), BF),
        scratch_shapes=[pltpu.VMEM((rows * cols // 1024, 8, 128), F32), pltpu.VMEM((8, 128), F32)],
        compiler_params=pltpu.CompilerParams(vmem_limit_bytes=24 * MIB),
        cost_estimate=pl.CostEstimate(flops=1_000_000_000, bytes_accessed=2 * MIB, transcendentals=0),
        name="merge_update",
    )(picks, scale, own, other, INV_LEFT3, INV_WIDE_HI, INV_WIDE_LO)


def on_device(weight, acts_t, out_grad, momentum, chosen, counts, steps):
    rows, cols = weight.shape
    islands = lax.axis_size("island")
    shards = lax.axis_size("shard")
    half = islands // 2
    same_core = [[2 * i + c for i in range(half)] for c in range(2)]
    other_core = [(i, i ^ 1) for i in range(islands)]
    momentum = momentum[0]

    picks = chosen[0] - lax.axis_index("shard") * (rows * cols // 128)
    live = counts[0]

    grad, squares = grad_call(acts_t, out_grad)
    squares = squares + lax.ppermute(squares, "shard", [(i, i ^ 1) for i in range(shards)])
    acts_grad = acts_grad_call(weight, out_grad)
    squares = squares + lax.ppermute(squares, "shard", [(i, i ^ 2) for i in range(shards)])
    coef_m, coef_g, pack_m, pack_g = coef_call(picks, live, momentum, grad)

    mean = squares[0, :1] / float(rows * cols * shards)
    factor = jnp.minimum(1.0, 1.0 / jnp.sqrt(mean + 1e-06))
    own_steps = steps.astype(F32)
    payload = (0.9 * pack_m + factor * pack_g) * own_steps
    meta = jnp.concatenate([picks.astype(F32), own_steps, jnp.zeros((111,), F32)])
    sent = jnp.concatenate([payload.reshape(1, PAY), meta[None]], 1)
    sent = jnp.broadcast_to(sent[None], (half, 1, PAY + 128))
    got = lax.all_to_all(sent, "island", 0, 0, tiled=True, axis_index_groups=same_core)
    swapped = lax.ppermute(got, "island", other_core)

    momentum_next = rest_call(picks, factor, coef_m, coef_g, momentum, grad)

    metas = jnp.concatenate([got[:, 0, PAY:PAY + 17], swapped[:, 0, PAY:PAY + 17]], 0)
    scale = (islands / jnp.sum(metas[:, 16]))[None]
    all_picks = metas[:, :16].astype(jnp.int32).reshape(-1)
    update = merge_call(
        all_picks, scale,
        got[:, 0, :PAY].reshape(half, SLOTS, 128),
        swapped[:, 0, :PAY].reshape(half, SLOTS, 128),
        rows, cols,
    )
    return (update, momentum_next[None], acts_grad)


def solution(mesh):
    placed = (
        P("shard", None),
        P("shard", "island"),
        P("island", None),
        P("island", "shard", None),
        P("island", "shard"),
        P("island", "shard"),
        P("island"),
    )
    return jax.shard_map(
        on_device,
        mesh=mesh,
        in_specs=placed,
        out_specs=(P("shard", None), P("island", "shard", None), P("shard", "island")),
        check_vma=False,
    )
```

time: 289 us -> 65.5 us (0.23)
  blocking collectives: 141 us -> 21.7 us
  local copies, waits for them, and re-layouts: 75.7 us -> 8.07 us
  waiting for transfers between devices: 24.7 us -> 0.01 us
  matrix products: 24.1 us -> 0 us
  Pallas kernels: 0 us -> 22.8 us
  between operations: 16.9 us -> 3.04 us
  starting transfers between devices: 0.04 us -> 8.62 us
  other arithmetic: 5.39 us -> 0.89 us
    psum x2 -> x0, blocking collectives: 141 us -> none  [the longest x1 131 us: on_device(): summed, total_steps = lax.psum((dense_grid, island_steps), 'island')]
    psum x1 -> x0, waiting for transfers between devices: 24.6 us -> none  [on_device(): summed, total_steps = lax.psum((dense_grid, island_steps), 'island')]
    dot_general x8 -> x0, matrix products: 24.1 us -> none  [the longest x3 10.7 us: apply_tiles(): jnp.einsum('ij,ajn->ain', left_side, strips, precision=lax.Precision.HIGH...]
    mul x2 -> x0, local copies, waits for them, and re-layouts: 23.1 us -> none  [on_device(): remaining = blocks * (1.0 - picked)[:, None]]
    pallas_call x0 -> x5, Pallas kernels: none -> 22.8 us  [the longest x1 12.8 us: merge_call(): pl.pallas_call(merge_kernel, in_specs=[sm, sm] + [vm] * 5, out_specs=vm,...]
    another operation x2 -> x0, local copies, waits for them, and re-layouts: 22.6 us -> none
    all_to_all x0 -> x1, blocking collectives: none -> 21.7 us  [on_device(): lax.all_to_all(sent, 'island', 0, 0, tiled=True, axis_index_groups=same_c...]
    transpose x2 -> x0, local copies, waits for them, and re-layouts: 19.6 us -> none  [the longest x1 11 us: to_blocks(): return shaped.transpose(0, 2, 1, 3).reshape(-1, 128)]
  transfers between devices with their start and end apart: 1 -> 3, of which waited for: 1 -> 0; matrix products, arithmetic and copies ran while one was open for 12% -> 3% of each run, Pallas kernels for 0% -> 12%
where the time goes in v1:
time: 65.5 us; the launch traced here: 65.1 us
  Pallas kernels  22.8 us (35%)
  blocking collectives  21.7 us (33%)
  starting transfers between devices  8.62 us (13%)
  local copies, waits for them, and re-layouts  8.07 us (12%)
  between operations  3.04 us (5%)
  other arithmetic  0.89 us (1%)
    all_to_all x1, blocking collectives, on_device(): lax.all_to_all(sent, 'island', 0, 0, tiled=True, axis_index_groups=same_c...  21.7 us
    pallas_call x1, Pallas kernels, merge_call(): pl.pallas_call(merge_kernel, in_specs=[sm, sm] + [vm] * 5, out_specs=vm,...  12.8 us
    unnamed x26, local copies, waits for them, and re-layouts  4.21 us
    ppermute x1, starting transfers between devices, on_device(): swapped = lax.ppermute(got, 'island', other_core)  3.95 us
    pallas_call x1, Pallas kernels, acts_grad_call(): pl.pallas_call(acts_grad_kernel, grid=(cols // chunk,), in_specs=[pl.Bloc...  3.34 us
    ppermute x1, starting transfers between devices, on_device(): lax.ppermute(squares, 'shard', [(i, i ^ 2) for i in range(shards)])  2.54 us
    pallas_call x1, Pallas kernels, rest_call(): pl.pallas_call(rest_kernel, in_specs=[sm, sm] + [vm] * 6, out_specs=vm, o...  2.44 us
    pallas_call x1, Pallas kernels, grad_call(): pl.pallas_call(grad_kernel, grid=(cols // chunk,), in_specs=[pl.BlockSpec...  2.41 us
  transfers between devices with their start and end apart: 3, of which 0 were waited for; matrix products, arithmetic and copies ran while one was open for 3% of the time, Pallas kernels for 12%

profile of v1, /device:TPU:1, one launch (start us, length us, event | category | flops | bytes accessed | tf_op | source)
XLA Modules:
  0.0 65.1 jit_solution(94031690867388698)
XLA Ops:
  0.6 0.0 copy-start
  0.6 2.2 %copy-done = bf16[256,8192]{1,0:T(8,128)(2,1)S(1)} copy-done((bf16[256,8192]{1,0:T(8,128)(2,1)S(1)}, bf16[256,8192]{1,0:T(8,128)(2,1)}, u32[]{:S(2)}) %copy-start) | copy-done | bytes 4194328
  2.8 0.8 %copy-done.6 = bf16[64,256]{1,0:T(8,128)(2,1)S(1)} copy-done((bf16[64,256]{1,0:T(8,128)(2,1)S(1)}, bf16[64,256]{1,0:T(8,128)(2,1)}, u32[]{:S(2)}) %copy-start.6) | copy-done | bytes 32792
  3.6 0.0 copy-start.9
  3.6 2.4 %weight_grad.1 = (f32[64,8192]{1,0:T(8,128)S(1)}, f32[1,128]{1,0:T(1,128)S(1)}) custom-call(bf16[64,256]{1,0:T(8,128)(2,1)S(1)} %copy-done.6, bf16[256,8192]{1,0:T(8,128)(2,1)S(1)} %copy-done), custom_call_target="tpu_custom_call" | custom-call | flops 268435456 | bytes 6291456 | tf_op jit(solution)/shard_map/weight_grad/pallas_call | solution.py:79
  6.0 2.1 %collective-permute-start = (f32[1,128]{1,0:T(1,128)S(1)}, f32[1,128]{1,0:T(1,128)S(1)}, u32[]{:S(2)}, u32[]{:S(2)}) collective-permute-start(f32[1,128]{1,0:T(1,128)S(1)} %get-tuple-element.11), channel_id=1, source_target_pairs={{0,1},{1,0},{2,3},{3,2},{4,5},{5,4},{6,7},{7,6},{8,9},{9,8},{10,11... | collective-permute-start | bytes 1544 | tf_op jit(solution)/shard_map/ppermute | solution.py:323
  8.8 0.0 copy-start.1
  8.8 0.1 maximum_bitcast_fusion
  9.7 0.0 collective-permute-done
  9.8 2.5 %collective-permute-start.1 = (f32[1,128]{1,0:T(1,128)S(1)}, f32[1,128]{1,0:T(1,128)S(1)}, u32[]{:S(2)}, u32[]{:S(2)}) collective-permute-start(f32[1,128]{1,0:T(1,128)S(1)} %add.13), channel_id=1, source_target_pairs={{0,2},{1,3},{2,0},{3,1},{4,6},{5,7},{6,4},{7,5},{8,10},{9,11},{10,... | collective-permute-start | bytes 1544 | tf_op jit(solution)/shard_map/ppermute | solution.py:325
  12.3 0.0 copy-done.8
  12.3 0.0 copy-start.7
  12.3 1.7 %selected_coefs.1 = (f32[128,128]{1,0:T(8,128)S(1)}, f32[128,128]{1,0:T(8,128)S(1)}, f32[16,128]{1,0:T(8,128)S(1)}, f32[16,128]{1,0:T(8,128)S(1)}) custom-call(s32[16]{0:T(128)S(1)} %get-tuple-element.16.picks, s32[1]{0:T(128)} %bitcast.18.counts, bf16[64,8192]{1,0:T(8,128)(2,1)S(1)} %bitcast.19, f32[64,8192]{1,0:T(8,128)S(1)} %get-tuple-element.9.grad, ...), custom_call_target="tpu_custom_call" | custom-call | flops 200000000 | bytes 3145728 | tf_op jit(solution)/shard_map/selected_coefs/pallas_call | solution.py:188
  14.1 0.0 collective-permute-done.1
  14.2 0.1 broadcast_in_dim.25
  14.4 21.7 %all_to_all.5 = f32[32,1,2176]{2,1,0:T(1,128)} all-to-all(f32[32,1,2176]{2,1,0:T(1,128)S(1)} %broadcast_in_dim.25), channel_id=1, replica_groups={{0,8,16,24,32,40,48,56,64,72,80,88,96,104,112,120,128,136,144,152,160,1..., dimensions={0} | all-to-all | bytes 557056 | tf_op jit(solution)/shard_map/all_to_all | solution.py:335
  36.0 4.0 %collective-permute-start.2 = (f32[32,1,2176]{2,1,0:T(1,128)}, f32[32,1,2176]{2,1,0:T(1,128)}, u32[]{:S(2)}, u32[]{:S(2)}) collective-permute-start(f32[32,1,2176]{2,1,0:T(1,128)} %all_to_all.5), channel_id=1, source_target_pairs={{0,4},{4,0},{8,12},{12,8},{16,20},{20,16},{24,28},{28,24},{32,36},... | collective-permute-start | bytes 835592 | tf_op jit(solution)/shard_map/ppermute | solution.py:336
  40.0 1.2 %copy-done.3 = bf16[64,8192]{1,0:T(8,128)(2,1)S(1)} copy-done((bf16[64,8192]{1,0:T(8,128)(2,1)S(1)}, bf16[64,8192]{1,0:T(8,128)(2,1)}, u32[]{:S(2)}) %copy-start.3) | copy-done | bytes 1048600
  41.2 3.3 %acts_grad.1 = bf16[64,256]{1,0:T(8,128)(2,1)} custom-call(bf16[64,8192]{1,0:T(8,128)(2,1)S(1)} %copy-done.3, bf16[256,8192]{1,0:T(8,128)(2,1)S(1)} %copy-done.1), custom_call_target="tpu_custom_call" | custom-call | flops 268435456 | bytes 5242880 | tf_op jit(solution)/shard_map/acts_grad/pallas_call | solution.py:120
  44.6 2.4 %momentum_rest.1 = bf16[64,8192]{1,0:T(8,128)(2,1)} custom-call(s32[16]{0:T(128)S(1)} %get-tuple-element.16.picks, f32[1]{0:T(128)} %bitcast.12.factor, f32[128,128]{1,0:T(8,128)S(1)} %get-tuple-element.13.coef_m, f32[128,128]{1,0:T(8,128)S(1)} %get-tuple-element.14.coef_g, bf16[64,8192]{1,0:T(8,128)(2,1)S(1)} %bitcast.20, ...), custom_call_target="tpu_custom_call" | custom-call | flops 100000000 | bytes 4194304 | tf_op jit(solution)/shard_map/momentum_rest/pallas_call | solution.py:239
  47.0 0.7 %slice.28 = f32[32,1,17]{2,1,0:T(1,128)S(1)} slice(f32[32,1,2176]{2,1,0:T(1,128)} %all_to_all.5), slice={[0:32], [0:1], [2048:2065]} | slice | bytes 4352 | tf_op jit(solution)/shard_map/slice | solution.py:340
  47.7 0.1 copy.17
  47.8 1.0 %slice.32 = f32[32,1,2048]{2,1,0:T(1,128)S(1)} slice(f32[32,1,2176]{2,1,0:T(1,128)} %all_to_all.5), slice={[0:32], [0:1], [0:2048]} | slice | bytes 524288 | tf_op jit(solution)/shard_map/slice | solution.py:345
  48.8 0.0 collective-permute-done.2
  48.8 0.7 %slice.29 = f32[32,1,17]{2,1,0:T(1,128)S(1)} slice(f32[32,1,2176]{2,1,0:T(1,128)} %collective-permute-done.2), slice={[0:32], [0:1], [2048:2065]} | slice | bytes 4352 | tf_op jit(solution)/shard_map/slice | solution.py:340
  49.5 0.1 copy.18
  49.6 0.7 %fusion.2 = f32[]{:T(128)} fusion(f32[32,17]{0,1:T(8,128)S(1)} %copy.18, f32[32,17]{0,1:T(8,128)S(1)} %copy.17), kind=kLoop, calls=%fused_computation.7 | loop fusion | flops 127 | bytes 4356 | tf_op jit(solution)/shard_map/reduce_sum | solution.py:341
  50.3 0.1 fusion.1
  50.4 0.1 copy.19
  50.5 0.1 reshape.28.picks
  51.2 1.0 %slice.33 = f32[32,1,2048]{2,1,0:T(1,128)S(1)} slice(f32[32,1,2176]{2,1,0:T(1,128)} %collective-permute-done.2), slice={[0:32], [0:1], [0:2048]} | slice | bytes 524288 | tf_op jit(solution)/shard_map/slice | solution.py:346
  52.2 12.8 %merge_update.1 = bf16[64,8192]{1,0:T(8,128)(2,1)} custom-call(s32[1024]{0:T(1024)S(1)} %reshape.28.picks, f32[1]{0:T(128)} %bitcast.9.scale, f32[32,16,128]{2,1,0:T(8,128)S(1)} %bitcast.21, f32[32,16,128]{2,1,0:T(8,128)S(1)} %bitcast.22, bf16[64,192]{1,0:T(8,128)(2,1)S(1)} %copy-done.7, bf16[256,256]{1,0:T(8,128)(2,1)S(1)} %copy-done.11, ...), custom_call_target="tpu_custom_call" | custom-call | flops 1000000000 | bytes 2097152 | tf_op jit(solution)/shard_map/merge_update/pallas_call | solution.py:298
  (24 shorter events, 0.1 us)
Async XLA Ops:
  0.6 2.2 %copy-start = (bf16[256,8192]{1,0:T(8,128)(2,1)S(1)}, bf16[256,8192]{1,0:T(8,128)(2,1)}, u32[]{:S(2)}) copy-start(bf16[256,8192]{1,0:T(8,128)(2,1)} %og.3) | copy-start | bytes 12582916
  2.8 0.8 %copy-start.6 = (bf16[64,256]{1,0:T(8,128)(2,1)S(1)}, bf16[64,256]{1,0:T(8,128)(2,1)}, u32[]{:S(2)}) copy-start(bf16[64,256]{1,0:T(8,128)(2,1)} %acts.1) | copy-start | bytes 98308
  3.6 5.2 %copy-start.12 = (s32[1,16]{1,0:T(1,128)S(1)}, s32[1,16]{1,0:T(1,128)}, u32[]{:S(2)}) copy-start(s32[1,16]{1,0:T(1,128)} %param.18) | copy-start | bytes 196
  3.6 8.7 %copy-start.2 = (bf16[1,64,8192]{2,1,0:T(8,128)(2,1)S(1)}, bf16[1,64,8192]{2,1,0:T(8,128)(2,1)}, u32[]{:S(2)}) copy-start(bf16[1,64,8192]{2,1,0:T(8,128)(2,1)} %param.17) | copy-start | bytes 3145732
  3.6 8.7 %copy-start.4 = (bf16[384,128]{1,0:T(8,128)(2,1)S(1)}, bf16[384,128]{1,0:T(8,128)(2,1)}, u32[]{:S(2)}) copy-start(bf16[384,128]{1,0:T(8,128)(2,1)} %constant.39.clone.right3) | copy-start | bytes 294916
  3.6 8.7 %copy-start.8 = (bf16[64,192]{1,0:T(8,128)(2,1)S(1)}, bf16[64,192]{1,0:T(8,128)(2,1)}, u32[]{:S(2)}) copy-start(bf16[64,192]{1,0:T(8,128)(2,1)} %constant.38.clone.left3) | copy-start | bytes 73732
  3.6 8.7 %copy-start.9 = (bf16[64,128]{1,0:T(8,128)(2,1)S(1)}, bf16[64,128]{1,0:T(8,128)(2,1)}, u32[]{:S(2)}) copy-start(bf16[64,128]{1,0:T(8,128)(2,1)} %constant.37.clone.left2) | copy-start | bytes 49156
  6.0 3.7 %collective-permute-start = (f32[1,128]{1,0:T(1,128)S(1)}, f32[1,128]{1,0:T(1,128)S(1)}, u32[]{:S(2)}, u32[]{:S(2)}) collective-permute-start(f32[1,128]{1,0:T(1,128)S(1)} %get-tuple-element.11), channel_id=1, source_target_pairs={{0,1},{1,0},{2,3},{3,2},{4,5},{5,4},{6,7},{7,6},{8,9},{9,8},{10,11... | collective-permute-start | bytes 1544 | tf_op jit(solution)/shard_map/ppermute | solution.py:323
  8.8 31.2 %copy-start.1 = (bf16[256,8192]{1,0:T(8,128)(2,1)S(1)}, bf16[256,8192]{1,0:T(8,128)(2,1)}, u32[]{:S(2)}) copy-start(bf16[256,8192]{1,0:T(8,128)(2,1)} %og.3) | copy-start | bytes 12582916
  9.8 4.3 %collective-permute-start.1 = (f32[1,128]{1,0:T(1,128)S(1)}, f32[1,128]{1,0:T(1,128)S(1)}, u32[]{:S(2)}, u32[]{:S(2)}) collective-permute-start(f32[1,128]{1,0:T(1,128)S(1)} %add.13), channel_id=1, source_target_pairs={{0,2},{1,3},{2,0},{3,1},{4,6},{5,7},{6,4},{7,5},{8,10},{9,11},{10,... | collective-permute-start | bytes 1544 | tf_op jit(solution)/shard_map/ppermute | solution.py:325
  12.3 32.3 %copy-start.7 = (bf16[64,192]{1,0:T(8,128)(2,1)S(1)}, bf16[64,192]{1,0:T(8,128)(2,1)}, u32[]{:S(2)}) copy-start(bf16[64,192]{1,0:T(8,128)(2,1)} %constant.40.clone.left3) | copy-start | bytes 73732
  36.0 12.8 %collective-permute-start.2 = (f32[32,1,2176]{2,1,0:T(1,128)}, f32[32,1,2176]{2,1,0:T(1,128)}, u32[]{:S(2)}, u32[]{:S(2)}) collective-permute-start(f32[32,1,2176]{2,1,0:T(1,128)} %all_to_all.5), channel_id=1, source_target_pairs={{0,4},{4,0},{8,12},{12,8},{16,20},{20,16},{24,28},{28,24},{32,36},... | collective-permute-start | bytes 835592 | tf_op jit(solution)/shard_map/ppermute | solution.py:336
  40.0 1.2 %copy-start.3 = (bf16[64,8192]{1,0:T(8,128)(2,1)S(1)}, bf16[64,8192]{1,0:T(8,128)(2,1)}, u32[]{:S(2)}) copy-start(bf16[64,8192]{1,0:T(8,128)(2,1)} %weight.1) | copy-start | bytes 3145732
  41.2 3.4 %copy-start.5 = (bf16[384,128]{1,0:T(8,128)(2,1)S(1)}, bf16[384,128]{1,0:T(8,128)(2,1)}, u32[]{:S(2)}) copy-start(bf16[384,128]{1,0:T(8,128)(2,1)} %constant.41.clone.right3) | copy-start | bytes 294916
  44.6 7.6 %copy-start.10 = (bf16[256,256]{1,0:T(8,128)(2,1)S(1)}, bf16[256,256]{1,0:T(8,128)(2,1)}, u32[]{:S(2)}) copy-start(bf16[256,256]{1,0:T(8,128)(2,1)} %constant.43.clone.wide_lo) | copy-start | bytes 393220
  44.6 7.6 %copy-start.11 = (bf16[256,256]{1,0:T(8,128)(2,1)S(1)}, bf16[256,256]{1,0:T(8,128)(2,1)}, u32[]{:S(2)}) copy-start(bf16[256,256]{1,0:T(8,128)(2,1)} %constant.42.clone.wide_hi) | copy-start | bytes 393220

commit v2 on v1

v2 whole, which is shorter than its diff:
```python
import functools

import jax
import jax.numpy as jnp
import ml_dtypes
import numpy as np
from jax import lax
from jax.experimental import pallas as pl
from jax.experimental.pallas import tpu as pltpu
from jax.sharding import PartitionSpec as P

BF = jnp.bfloat16
F32 = jnp.float32
SLOTS = 16
PAY = SLOTS * 128
MIB = 1 << 20


def dct_matrix():
    freq = np.arange(64, dtype=np.float64)[:, None]
    place = np.arange(64, dtype=np.float64)[None, :]
    waves = np.cos(np.pi * (2.0 * place + 1.0) * freq / 128.0)
    return np.where(freq == 0.0, 0.125, np.sqrt(2.0 / 64.0)) * waves


def halves(a):
    hi = a.astype(ml_dtypes.bfloat16)
    lo = (a - hi.astype(np.float64)).astype(ml_dtypes.bfloat16)
    return hi, lo


COS = dct_matrix()
COS_HI, COS_LO = halves(COS)
INV_HI, INV_LO = halves(COS.T)


def diagonal(a, copies):
    return np.kron(np.eye(copies), a.astype(np.float64)).astype(ml_dtypes.bfloat16)


FWD_LEFT3 = np.concatenate([COS_HI, COS_HI, COS_LO], 1)
FWD_LEFT2 = np.concatenate([COS_HI, COS_LO], 1)
INV_LEFT3 = np.concatenate([INV_HI, INV_HI, INV_LO], 1)
FWD_RIGHT3 = np.concatenate([diagonal(COS_HI.T, 2), diagonal(COS_HI.T, 2), diagonal(COS_LO.T, 2)], 0)
INV_RIGHT3 = np.concatenate([diagonal(COS_HI, 2), diagonal(COS_HI, 2), diagonal(COS_LO, 2)], 0)
INV_WIDE_HI = diagonal(COS_HI, 4)
INV_WIDE_LO = diagonal(COS_LO, 4)


def split(x):
    hi = x.astype(BF)
    return hi, (x - hi.astype(F32)).astype(BF)


def dot(a, b):
    return jnp.dot(a, b, preferred_element_type=F32)


PARTS = 2


def grad_kernel(acts, og, weight, grad, squares, og_in, weight_in, acts_in, sem):
    cols = og_in.shape[1]
    width = cols // PARTS
    first = pltpu.make_async_copy(acts, acts_in, sem.at[PARTS])
    first.start()
    parts = []
    for i in range(PARTS):
        at = slice(i * width, (i + 1) * width)
        parts.append(pltpu.make_async_copy(og.at[:, at], og_in.at[:, at], sem.at[i]))
        parts[i].start()
    last = pltpu.make_async_copy(weight, weight_in, sem.at[PARTS + 1])
    last.start()
    first.wait()
    a = acts_in[...]
    total = jnp.zeros((8, 512), F32)
    for i in range(PARTS):
        at = slice(i * width, (i + 1) * width)
        parts[i].wait()
        g = dot(a, og_in[:, at])
        grad[:, at] = g
        g = jnp.sum((g * g).reshape(-1, 8, width), axis=0)
        for k in range(0, width, 512):
            total = total + g[:, k:k + 512]
    squares[...] = jnp.full(squares.shape, jnp.sum(total), F32)
    last.wait()


def grad_call(acts, og, weight):
    rows, toks = acts.shape
    cols = og.shape[1]
    vm = pl.BlockSpec(memory_space=pltpu.VMEM)
    anyw = pl.BlockSpec(memory_space=pl.ANY)
    held = [pltpu.with_memory_space_constraint(x, pltpu.HBM) for x in (acts, og, weight)]
    return pl.pallas_call(
        grad_kernel,
        in_specs=[anyw] * 3,
        out_specs=[vm] * 4,
        out_shape=[
            jax.ShapeDtypeStruct((rows, cols), F32),
            jax.ShapeDtypeStruct((1, 128), F32),
            jax.ShapeDtypeStruct((toks, cols), BF),
            jax.ShapeDtypeStruct((rows, cols), BF),
        ],
        scratch_shapes=[
            pltpu.VMEM((rows, toks), BF),
            pltpu.SemaphoreType.DMA((PARTS + 2,)),
        ],
        compiler_params=pltpu.CompilerParams(vmem_limit_bytes=24 * MIB),
        cost_estimate=pl.CostEstimate(flops=2 * rows * toks * cols, bytes_accessed=6 * MIB, transcendentals=0),
        name="weight_grad",
    )(*held)


def acts_grad_kernel(weight, og, out):
    total = lax.dot_general(og[...], weight[...], (((1,), (1,)), ((), ())), preferred_element_type=F32)
    out[...] = total.T.astype(BF)


def acts_grad_call(weight, og):
    rows, cols = weight.shape
    toks = og.shape[0]
    vm = pl.BlockSpec(memory_space=pltpu.VMEM)
    return pl.pallas_call(
        acts_grad_kernel,
        in_specs=[vm, vm],
        out_specs=vm,
        out_shape=jax.ShapeDtypeStruct((rows, toks), BF),
        compiler_params=pltpu.CompilerParams(vmem_limit_bytes=16 * MIB),
        cost_estimate=pl.CostEstimate(flops=2 * rows * toks * cols, bytes_accessed=5 * MIB, transcendentals=0),
        name="acts_grad",
    )(weight, og)


def lane_group(shape):
    return lax.broadcasted_iota(jnp.int32, shape, 1) >> 4


def coef_kernel(picks, counts, momentum, grad, left2, left3, right3, back_left3, back_right3,
                pack_m, pack_g, rest_m, rest_g,
                mom_in, grad_in, side_m, side_g, low, wide):
    pairs = [(picks[j] >> 3) & 63 for j in range(SLOTS)]
    lanes = [pl.ds(pl.multiple_of(p * 128, 128), 128) for p in pairs]
    tops = [pl.ds(pl.multiple_of((picks[j] >> 9) * 8, 8), 8) for j in range(SLOTS)]
    offs = [picks[j] & 7 for j in range(SLOTS)]
    here = [slice(128 * j, 128 * j + 128) for j in range(SLOTS)]
    for j in range(SLOTS):
        mom_in[:, here[j]] = momentum[:, lanes[j]]
        grad_in[:, here[j]] = grad[:, lanes[j]]
    wide[...] = jnp.zeros_like(wide)
    m = mom_in[...]
    g_hi, g_lo = split(grad_in[...])
    side_m[...] = dot(left2[...], jnp.concatenate([m, m], 0))
    side_g[...] = dot(left3[...], jnp.concatenate([g_hi, g_lo, g_hi], 0))
    for j in range(SLOTS):
        low[8 * j:8 * j + 8, :] = side_m[tops[j], here[j]]
        low[128 + 8 * j:136 + 8 * j, :] = side_g[tops[j], here[j]]
    hi, lo = split(low[...])
    low[...] = dot(jnp.concatenate([hi, lo, hi], 1), right3[...])
    group = lane_group((8, 128))
    live = counts[0]
    wants = [jnp.where(j < live, offs[j], 8) for j in range(SLOTS)]
    for base, pack in ((0, pack_m), (128, pack_g)):
        packed = [jnp.zeros((8, 128), F32)] * 2
        for j in range(SLOTS):
            at = slice(base + 8 * j, base + 8 * j + 8)
            kept = jnp.where(group == wants[j], low[at, :], 0.0)
            low[at, :] = kept
            packed[j // 8] = packed[j // 8] + pltpu.roll(kept, ((j % 8 - offs[j]) & 7) * 16, 1)
        pack[0:8, :] = packed[0]
        pack[8:16, :] = packed[1]
    hi, lo = split(low[...])
    low[...] = dot(jnp.concatenate([hi, lo, hi], 1), back_right3[...])
    for j in range(SLOTS):
        wide[tops[j], 128 * j:128 * j + 128] = low[8 * j:8 * j + 8, :]
        wide[tops[j], PAY + 128 * j:PAY + 128 * j + 128] = low[128 + 8 * j:136 + 8 * j, :]
    hi, lo = split(wide[...])
    wide[...] = dot(back_left3[...], jnp.concatenate([hi, lo, hi], 0))
    cols = grad.shape[1]
    for c in range(0, cols, 1024):
        at = slice(c, c + 1024)
        rest_m[:, at] = 0.9 * momentum[:, at].astype(F32)
        rest_g[:, at] = grad[:, at]
    for j in range(SLOTS):
        rest_m[:, lanes[j]] = rest_m[:, lanes[j]] - 0.9 * wide[:, 128 * j:128 * j + 128]
        rest_g[:, lanes[j]] = rest_g[:, lanes[j]] - wide[:, PAY + 128 * j:PAY + 128 * j + 128]


def coef_call(picks, counts, momentum, grad):
    rows, cols = grad.shape
    vm = pl.BlockSpec(memory_space=pltpu.VMEM)
    sm = pl.BlockSpec(memory_space=pltpu.SMEM)
    return pl.pallas_call(
        coef_kernel,
        in_specs=[sm, sm] + [vm] * 7,
        out_specs=[vm] * 4,
        out_shape=[
            jax.ShapeDtypeStruct((16, 128), F32),
            jax.ShapeDtypeStruct((16, 128), F32),
            jax.ShapeDtypeStruct((rows, cols), F32),
            jax.ShapeDtypeStruct((rows, cols), F32),
        ],
        scratch_shapes=[
            pltpu.VMEM((rows, PAY), BF),
            pltpu.VMEM((rows, PAY), F32),
            pltpu.VMEM((rows, PAY), F32),
            pltpu.VMEM((rows, PAY), F32),
            pltpu.VMEM((256, 128), F32),
            pltpu.VMEM((rows, 2 * PAY), F32),
        ],
        compiler_params=pltpu.CompilerParams(vmem_limit_bytes=24 * MIB),
        cost_estimate=pl.CostEstimate(flops=300_000_000, bytes_accessed=8 * MIB, transcendentals=0),
        name="selected_coefs",
    )(picks, counts, momentum, grad, FWD_LEFT2, FWD_LEFT3, FWD_RIGHT3, INV_LEFT3, INV_RIGHT3)


GROUP = 16


def add_islands(got, grid, ints, picks, sem):
    ints[...] = got[:, :, PAY:].astype(jnp.int32)
    to_scalars = pltpu.make_async_copy(ints, picks, sem)
    to_scalars.start()
    grid[...] = jnp.zeros_like(grid)
    steps = jnp.sum(got[:, :, PAY + SLOTS:PAY + SLOTS + 1])
    to_scalars.wait()
    group = lane_group((8, 128))

    def one(i, carry):
        tiles = [got[i, 0, 1024 * t:1024 * t + 1024].reshape(8, 128) for t in range(2)]
        olds, news, masks, places = [], [], [], []
        for j in range(SLOTS):
            b = picks[i, 0, j]
            off = b & 7
            place = b >> 3
            news.append(pltpu.roll(tiles[j // 8], ((off - j % 8) & 7) * 16, 1))
            olds.append(grid[place])
            masks.append(group == off)
            places.append(place)
        for j in range(SLOTS):
            pltpu.store(grid.at[places[j]], olds[j] + news[j], mask=masks[j])
        return carry

    lax.fori_loop(0, got.shape[0], one, 0, unroll=4)
    return steps


def scatter_kernel(got, grid, steps, ints, picks, sem):
    steps[...] = jnp.full(steps.shape, add_islands(got, grid, ints, picks, sem), F32)


def scatter_call(got, rows, cols):
    vm = pl.BlockSpec(memory_space=pltpu.VMEM)
    islands = got.shape[0]
    return pl.pallas_call(
        scatter_kernel,
        in_specs=[vm],
        out_specs=[vm, vm],
        out_shape=[
            jax.ShapeDtypeStruct((rows * cols // 1024, 8, 128), F32),
            jax.ShapeDtypeStruct((1, 128), F32),
        ],
        scratch_shapes=[
            pltpu.VMEM((islands, 1, 128), jnp.int32),
            pltpu.SMEM((islands, 1, 128), jnp.int32),
            pltpu.SemaphoreType.DMA,
        ],
        compiler_params=pltpu.CompilerParams(vmem_limit_bytes=16 * MIB),
        cost_estimate=pl.CostEstimate(flops=300_000_000, bytes_accessed=8 * MIB, transcendentals=0),
        name="scatter_own",
    )(got)


def merge_kernel(got, first, first_steps, left3, wide_hi, wide_lo, out, grid, ints, picks, done, sem, out_sem):
    islands = 2.0 * got.shape[0]
    steps = add_islands(got, grid, ints, picks, sem)
    s = islands / (steps + first_steps[0, 0])
    pairs = grid.shape[0] // 8
    width = 256 * GROUP
    copies = []
    for q in range(pairs // (2 * GROUP)):
        parts = []
        for k in range(2 * GROUP):
            at = [r * pairs + 2 * GROUP * q + k for r in range(8)]
            parts.append(jnp.concatenate([grid[p] + first[p] for p in at], 0))
        hi, lo = split(jnp.concatenate(parts, 1))
        z = dot(left3[...], jnp.concatenate([hi, lo, hi], 0)) * s
        z = jnp.concatenate([z[:, 256 * k:256 * k + 256] for k in range(GROUP)], 0)
        hi, lo = split(z)
        y = dot(hi, wide_hi[...]) + (dot(lo, wide_hi[...]) + dot(hi, wide_lo[...]))
        y = y.astype(BF)
        for k in range(GROUP):
            at = 256 * (GROUP * q + k)
            done[:, at:at + 256] = y[64 * k:64 * k + 64]
        at = slice(width * q, width * q + width)
        copies.append(pltpu.make_async_copy(done.at[:, at], out.at[:, at], out_sem.at[q]))
        copies[q].start()
    for c in copies:
        c.wait()


def merge_call(got, first, first_steps, rows, cols):
    vm = pl.BlockSpec(memory_space=pltpu.VMEM)
    anyw = pl.BlockSpec(memory_space=pl.ANY)
    islands = got.shape[0]
    return pl.pallas_call(
        merge_kernel,
        in_specs=[vm] * 6,
        out_specs=anyw,
        out_shape=jax.ShapeDtypeStruct((rows, cols), BF),
        scratch_shapes=[
            pltpu.VMEM((rows * cols // 1024, 8, 128), F32),
            pltpu.VMEM((islands, 1, 128), jnp.int32),
            pltpu.SMEM((islands, 1, 128), jnp.int32),
            pltpu.VMEM((rows, cols), BF),
            pltpu.SemaphoreType.DMA,
            pltpu.SemaphoreType.DMA((cols // (256 * GROUP),)),
        ],
        compiler_params=pltpu.CompilerParams(vmem_limit_bytes=32 * MIB),
        cost_estimate=pl.CostEstimate(flops=1_000_000_000, bytes_accessed=2 * MIB, transcendentals=0),
        name="merge_update",
    )(got, first, first_steps, INV_LEFT3, INV_WIDE_HI, INV_WIDE_LO)


def on_device(weight, acts_t, out_grad, momentum, chosen, counts, steps):
    rows, cols = weight.shape
    islands = lax.axis_size("island")
    shards = lax.axis_size("shard")
    half = islands // 2
    same_core = [[2 * i + c for i in range(half)] for c in range(2)]
    other_core = [(i, i ^ 1) for i in range(islands)]
    momentum = momentum[0]

    picks = chosen[0] % (rows * cols // 128)
    live = counts[0]

    grad, squares, og_held, weight_held = grad_call(acts_t, out_grad, weight)
    squares = squares + lax.ppermute(squares, "shard", [(i, i ^ 1) for i in range(shards)])
    acts_grad = acts_grad_call(weight_held, og_held)
    squares, acts_grad = lax.optimization_barrier((squares, acts_grad))
    squares = squares + lax.ppermute(squares, "shard", [(i, i ^ 3) for i in range(shards)])
    coefs = coef_call(picks, live, momentum, grad)
    squares, coefs = lax.optimization_barrier((squares, coefs))
    pack_m, pack_g, rest_m, rest_g = coefs

    mean = squares[0, :1] / float(rows * cols * shards)
    factor = jnp.minimum(1.0, 1.0 / jnp.sqrt(mean + 1e-06))
    own_steps = steps.astype(F32)
    payload = (0.9 * pack_m + factor * pack_g) * own_steps
    meta = jnp.concatenate([picks.astype(F32), own_steps, jnp.zeros((111,), F32)])
    sent = jnp.concatenate([payload.reshape(1, PAY), meta[None]], 1)
    sent = jnp.broadcast_to(sent[None], (half, 1, PAY + 128))
    got = lax.all_to_all(sent, "island", 0, 0, tiled=True, axis_index_groups=same_core)
    swapped = lax.ppermute(got, "island", other_core)

    momentum_next = (rest_m + factor * rest_g).astype(BF)
    first, first_steps = scatter_call(got, rows, cols)
    update = merge_call(swapped, first, first_steps, rows, cols)
    return (update, momentum_next[None], acts_grad)


def solution(mesh):
    placed = (
        P("shard", None),
        P("shard", "island"),
        P("island", None),
        P("island", "shard", None),
        P("island", "shard"),
        P("island", "shard"),
        P("island"),
    )
    return jax.shard_map(
        on_device,
        mesh=mesh,
        in_specs=placed,
        out_specs=(P("shard", None), P("island", "shard", None), P("shard", "island")),
        check_vma=False,
    )
```

time: 65.5 us -> 48.6 us (0.74)
  local copies, waits for them, and re-layouts: 8.07 us -> 0.19 us
  Pallas kernels: 22.8 us -> 15.3 us
  between operations: 3.04 us -> 2.18 us
    pallas_call x5, Pallas kernels: 22.8 us -> 15.3 us  [the longest x1 5.47 us: merge_call(): pl.pallas_call(merge_kernel, in_specs=[vm] * 6, out_specs=anyw, out_shape...]
    unnamed x26 -> x18, local copies, waits for them, and re-layouts: 4.21 us -> 0.04 us
    slice x4 -> x0, local copies, waits for them, and re-layouts: 3.38 us -> none  [the longest x1 0.97 us: on_device(): got[:, 0, :PAY].reshape(half, SLOTS, 128)]
    broadcast_in_dim x0 -> x1, other arithmetic: none -> 1.16 us  [on_device(): return (update, momentum_next[None], acts_grad)]
    reduce_sum x1 -> x0, other arithmetic: 0.68 us -> none  [on_device(): scale = (islands / jnp.sum(metas[:, 16]))[None]]
  transfers between devices with their start and end apart: 3 -> 3, of which waited for: 0 -> 0; matrix products, arithmetic and copies ran while one was open for 3% -> 3% of each run, Pallas kernels for 12% -> 14%
where the time goes in v2:
time: 48.6 us; the launch traced here: 48.5 us
  blocking collectives  21.5 us (44%)
  Pallas kernels  15.3 us (31%)
  starting transfers between devices  7.98 us (16%)
  between operations  2.18 us (4%)
  other arithmetic  1.3 us (3%)
    all_to_all x1, blocking collectives, on_device(): lax.all_to_all(sent, 'island', 0, 0, tiled=True, axis_index_groups=same_c...  21.5 us
    pallas_call x1, Pallas kernels, merge_call(): pl.pallas_call(merge_kernel, in_specs=[vm] * 6, out_specs=anyw, out_shape...  5.47 us
    ppermute x1, starting transfers between devices, on_device(): swapped = lax.ppermute(got, 'island', other_core)  3.95 us
    pallas_call x1, Pallas kernels, scatter_call(): pl.pallas_call(scatter_kernel, in_specs=[vm], out_specs=[vm, vm], out_sha...  3.02 us
    pallas_call x1, Pallas kernels, grad_call(): pl.pallas_call(grad_kernel, in_specs=[anyw] * 3, out_specs=[vm] * 4, out_...  2.89 us
    ppermute x1, starting transfers between devices, on_device(): lax.ppermute(squares, 'shard', [(i, i ^ 1) for i in range(shards)])  2.13 us
    pallas_call x1, Pallas kernels, coef_call(): pl.pallas_call(coef_kernel, in_specs=[sm, sm] + [vm] * 7, out_specs=[vm]...  1.99 us
    ppermute x1, starting transfers between devices, on_device(): lax.ppermute(squares, 'shard', [(i, i ^ 3) for i in range(shards)])  1.9 us
  transfers between devices with their start and end apart: 3, of which 0 were waited for; matrix products, arithmetic and copies ran while one was open for 3% of the time, Pallas kernels for 14%

profile of v2, /device:TPU:1, one launch (start us, length us, event | category | flops | bytes accessed | tf_op | source)
XLA Modules:
  0.0 48.5 jit_solution(14556921563283122474)
XLA Ops:
  0.6 0.0 copy-start.8
  0.6 2.9 %weight_grad.1 = (f32[64,8192]{1,0:T(8,128)S(1)}, f32[1,128]{1,0:T(1,128)S(1)}, bf16[256,8192]{1,0:T(8,128)(2,1)S(1)}, bf16[64,8192]{1,0:T(8,128)(2,1)S(1)}) custom-call(bf16[64,256]{1,0:T(8,128)(2,1)} %acts.1, bf16[256,8192]{1,0:T(8,128)(2,1)} %og.1, bf16[64,8192]{1,0:T(8,128)(2,1)} %weight.1), custom_call_target="tpu_custom_call" | custom-call | flops 268435456 | bytes 6291456 | tf_op jit(solution)/shard_map/weight_grad/pallas_call | solution.py:95
  3.5 2.1 %collective-permute-start = (f32[1,128]{1,0:T(1,128)S(1)}, f32[1,128]{1,0:T(1,128)S(1)}, u32[]{:S(2)}, u32[]{:S(2)}) collective-permute-start(f32[1,128]{1,0:T(1,128)S(1)} %get-tuple-element.20), channel_id=1, source_target_pairs={{0,1},{1,0},{2,3},{3,2},{4,5},{5,4},{6,7},{7,6},{8,9},{9,8},{10,11... | collective-permute-start | bytes 1544 | tf_op jit(solution)/shard_map/ppermute | solution.py:338
  5.7 0.0 copy-done.8
  6.3 0.1 maximum_bitcast_fusion
  6.4 0.0 copy-start
  6.4 0.0 copy-start.1
  6.4 0.0 copy-start.4
  6.4 0.0 copy-start.5
  6.4 0.0 copy-start.6
  6.4 0.0 copy-start.7
  6.5 1.9 %acts_grad.1 = bf16[64,256]{1,0:T(8,128)(2,1)} custom-call(bf16[64,8192]{1,0:T(8,128)(2,1)S(1)} %get-tuple-element.21.weight, bf16[256,8192]{1,0:T(8,128)(2,1)S(1)} %get-tuple-element.22.og), custom_call_target="tpu_custom_call" | custom-call | flops 268435456 | bytes 5242880 | tf_op jit(solution)/shard_map/acts_grad/pallas_call | solution.py:124
  9.0 0.0 collective-permute-done
  9.0 1.9 %collective-permute-start.1 = (f32[1,128]{1,0:T(1,128)S(1)}, f32[1,128]{1,0:T(1,128)S(1)}, u32[]{:S(2)}, u32[]{:S(2)}) collective-permute-start(f32[1,128]{1,0:T(1,128)S(1)} %add.22), channel_id=1, source_target_pairs={{0,3},{1,2},{2,1},{3,0},{4,7},{5,6},{6,5},{7,4},{8,11},{9,10},{10,... | collective-permute-start | bytes 1544 | tf_op jit(solution)/shard_map/ppermute | solution.py:341
  10.9 0.0 copy-done
  10.9 0.0 copy-done.1
  10.9 0.0 copy-done.4
  10.9 0.0 copy-done.5
  11.0 0.0 copy-done.6
  11.0 0.0 copy-done.7
  11.0 2.0 %selected_coefs.1 = (f32[16,128]{1,0:T(8,128)S(1)}, f32[16,128]{1,0:T(8,128)S(1)}, f32[64,8192]{1,0:T(8,128)S(1)}, f32[64,8192]{1,0:T(8,128)S(1)}) custom-call(s32[16]{0:T(128)S(1)} %get-tuple-element.38.picks, s32[1]{0:T(128)} %bitcast.13.counts, bf16[64,8192]{1,0:T(8,128)(2,1)S(1)} %bitcast.14, f32[64,8192]{1,0:T(8,128)S(1)} %get-tuple-element.24.grad, ...), custom_call_target="tpu_custom_call" | custom-call | flops 300000000 | bytes 8388608 | tf_op jit(solution)/shard_map/selected_coefs/pallas_call | solution.py:193
  13.0 0.0 collective-permute-done.1
  13.1 0.1 broadcast_in_dim.23
  13.3 21.5 %all_to_all.5.got = f32[32,1,2176]{2,1,0:T(1,128)S(1)} all-to-all(f32[32,1,2176]{2,1,0:T(1,128)S(1)} %broadcast_in_dim.23), channel_id=1, replica_groups={{0,8,16,24,32,40,48,56,64,72,80,88,96,104,112,120,128,136,144,152,160,1..., dimensions={0} | all-to-all | bytes 557056 | tf_op jit(solution)/shard_map/all_to_all | solution.py:353
  34.8 0.0 copy-start.2
  34.8 4.0 %collective-permute-start.2 = (f32[32,1,2176]{2,1,0:T(1,128)S(1)}, f32[32,1,2176]{2,1,0:T(1,128)S(1)}, u32[]{:S(2)}, u32[]{:S(2)}) collective-permute-start(f32[32,1,2176]{2,1,0:T(1,128)S(1)} %all_to_all.5.got), channel_id=1, source_target_pairs={{0,4},{4,0},{8,12},{12,8},{16,20},{20,16},{24,28},{28,24},{32,36},... | collective-permute-start | bytes 835592 | tf_op jit(solution)/shard_map/ppermute | solution.py:354
  38.8 1.2 %fusion = bf16[1,64,8192]{2,1,0:T(8,128)(2,1)} fusion(f32[64,8192]{1,0:T(8,128)S(1)} %get-tuple-element.34, f32[64,8192]{1,0:T(8,128)S(1)} %get-tuple-element.35, f32[]{:T(128)} %bitcast.3), kind=kLoop, calls=%fused_computation.1 | loop fusion | flops 1572864 | bytes 5242884 | tf_op jit(solution)/shard_map/broadcast_in_dim | solution.py:359
  39.9 3.0 %scatter_own.1 = (f32[512,8,128]{2,1,0:T(8,128)S(1)}, f32[1,128]{1,0:T(1,128)S(1)}) custom-call(f32[32,1,2176]{2,1,0:T(1,128)S(1)} %all_to_all.5.got), custom_call_target="tpu_custom_call" | custom-call | flops 300000000 | bytes 8388608 | tf_op jit(solution)/shard_map/scatter_own/pallas_call | solution.py:255
  43.0 0.0 collective-permute-done.2.got
  43.0 0.0 copy-done.2
  43.0 0.0 copy-done.3
  43.0 5.5 %merge_update.1 = bf16[64,8192]{1,0:T(8,128)(2,1)} custom-call(f32[32,1,2176]{2,1,0:T(1,128)S(1)} %collective-permute-done.2.got, f32[512,8,128]{2,1,0:T(8,128)S(1)} %get-tuple-element.32.first, f32[1,128]{1,0:T(1,128)S(1)} %get-tuple-element.33.first_steps, bf16[64,192]{1,0:T(8,128)(2,1)S(1)} %copy-done.1, bf16[256,256]{1,0:T(8,128)(2,1)S(1)} %copy-done.2, ...), custom_call_target="tpu_custom_call" | custom-call | flops 1000000000 | bytes 2097152 | tf_op jit(solution)/shard_map/merge_update/pallas_call | solution.py:306
  (7 shorter events, 0.1 us)
Async XLA Ops:
  0.6 5.0 %copy-start.8 = (s32[1,16]{1,0:T(1,128)S(1)}, s32[1,16]{1,0:T(1,128)}, u32[]{:S(2)}) copy-start(s32[1,16]{1,0:T(1,128)} %param.18) | copy-start | bytes 196
  3.5 5.5 %collective-permute-start = (f32[1,128]{1,0:T(1,128)S(1)}, f32[1,128]{1,0:T(1,128)S(1)}, u32[]{:S(2)}, u32[]{:S(2)}) collective-permute-start(f32[1,128]{1,0:T(1,128)S(1)} %get-tuple-element.20), channel_id=1, source_target_pairs={{0,1},{1,0},{2,3},{3,2},{4,5},{5,4},{6,7},{7,6},{8,9},{9,8},{10,11... | collective-permute-start | bytes 1544 | tf_op jit(solution)/shard_map/ppermute | solution.py:338
  6.4 4.5 %copy-start = (bf16[1,64,8192]{2,1,0:T(8,128)(2,1)S(1)}, bf16[1,64,8192]{2,1,0:T(8,128)(2,1)}, u32[]{:S(2)}) copy-start(bf16[1,64,8192]{2,1,0:T(8,128)(2,1)} %param.17) | copy-start | bytes 3145732
  6.4 4.5 %copy-start.1 = (bf16[64,192]{1,0:T(8,128)(2,1)S(1)}, bf16[64,192]{1,0:T(8,128)(2,1)}, u32[]{:S(2)}) copy-start(bf16[64,192]{1,0:T(8,128)(2,1)} %constant.46.clone.back_left3.left3) | copy-start | bytes 73732
  6.4 4.5 %copy-start.4 = (bf16[384,128]{1,0:T(8,128)(2,1)S(1)}, bf16[384,128]{1,0:T(8,128)(2,1)}, u32[]{:S(2)}) copy-start(bf16[384,128]{1,0:T(8,128)(2,1)} %constant.45.clone.right3) | copy-start | bytes 294916
  6.4 4.5 %copy-start.5 = (bf16[384,128]{1,0:T(8,128)(2,1)S(1)}, bf16[384,128]{1,0:T(8,128)(2,1)}, u32[]{:S(2)}) copy-start(bf16[384,128]{1,0:T(8,128)(2,1)} %constant.47.clone.back_right3) | copy-start | bytes 294916
  6.4 4.5 %copy-start.6 = (bf16[64,192]{1,0:T(8,128)(2,1)S(1)}, bf16[64,192]{1,0:T(8,128)(2,1)}, u32[]{:S(2)}) copy-start(bf16[64,192]{1,0:T(8,128)(2,1)} %constant.44.clone.left3) | copy-start | bytes 73732
  6.4 4.5 %copy-start.7 = (bf16[64,128]{1,0:T(8,128)(2,1)S(1)}, bf16[64,128]{1,0:T(8,128)(2,1)}, u32[]{:S(2)}) copy-start(bf16[64,128]{1,0:T(8,128)(2,1)} %constant.43.clone.left2) | copy-start | bytes 49156
  9.0 3.9 %collective-permute-start.1 = (f32[1,128]{1,0:T(1,128)S(1)}, f32[1,128]{1,0:T(1,128)S(1)}, u32[]{:S(2)}, u32[]{:S(2)}) collective-permute-start(f32[1,128]{1,0:T(1,128)S(1)} %add.22), channel_id=1, source_target_pairs={{0,3},{1,2},{2,1},{3,0},{4,7},{5,6},{6,5},{7,4},{8,11},{9,10},{10,... | collective-permute-start | bytes 1544 | tf_op jit(solution)/shard_map/ppermute | solution.py:341
  34.8 8.2 %copy-start.2 = (bf16[256,256]{1,0:T(8,128)(2,1)S(1)}, bf16[256,256]{1,0:T(8,128)(2,1)}, u32[]{:S(2)}) copy-start(bf16[256,256]{1,0:T(8,128)(2,1)} %constant.48.clone.wide_hi) | copy-start | bytes 393220
  34.8 8.2 %copy-start.3 = (bf16[256,256]{1,0:T(8,128)(2,1)S(1)}, bf16[256,256]{1,0:T(8,128)(2,1)}, u32[]{:S(2)}) copy-start(bf16[256,256]{1,0:T(8,128)(2,1)} %constant.49.clone.wide_lo) | copy-start | bytes 393220
  34.8 8.2 %collective-permute-start.2 = (f32[32,1,2176]{2,1,0:T(1,128)S(1)}, f32[32,1,2176]{2,1,0:T(1,128)S(1)}, u32[]{:S(2)}, u32[]{:S(2)}) collective-permute-start(f32[32,1,2176]{2,1,0:T(1,128)S(1)} %all_to_all.5.got), channel_id=1, source_target_pairs={{0,4},{4,0},{8,12},{12,8},{16,20},{20,16},{24,28},{28,24},{32,36},... | collective-permute-start | bytes 835592 | tf_op jit(solution)/shard_map/ppermute | solution.py:354

commit v3 on v2

--- a/solution.py
+++ b/solution.py
@@ -43,8 +43,10 @@
 INV_LEFT3 = np.concatenate([INV_HI, INV_HI, INV_LO], 1)
 FWD_RIGHT3 = np.concatenate([diagonal(COS_HI.T, 2), diagonal(COS_HI.T, 2), diagonal(COS_LO.T, 2)], 0)
 INV_RIGHT3 = np.concatenate([diagonal(COS_HI, 2), diagonal(COS_HI, 2), diagonal(COS_LO, 2)], 0)
-INV_WIDE_HI = diagonal(COS_HI, 4)
-INV_WIDE_LO = diagonal(COS_LO, 4)
+INV_RIGHT2 = np.block([
+    [diagonal(COS_HI, 2), diagonal(COS_LO, 2)],
+    [diagonal(COS_HI, 2), np.zeros((128, 128), ml_dtypes.bfloat16)],
+])
 
 
 def split(x):
@@ -214,67 +216,98 @@
     )(picks, counts, momentum, grad, FWD_LEFT2, FWD_LEFT3, FWD_RIGHT3, INV_LEFT3, INV_RIGHT3)
 
 
-GROUP = 16
-
-
-def add_islands(got, grid, ints, picks, sem):
-    ints[...] = got[:, :, PAY:].astype(jnp.int32)
+GROUP = 8
+SHARE = 4
+
+
+def gather_meta(got, ints, picks, sem):
+    rows = []
+    for a in range(got.shape[0] // SHARE):
+        turned = [got[SHARE * a + k, :, PAY:] for k in range(SHARE)]
+        turned = [turned[0]] + [pltpu.roll(turned[k], 32 * k, 1) for k in range(1, SHARE)]
+        rows.append(sum(turned))
+    rows = jnp.concatenate(rows, 0)
+    ints[...] = rows.astype(jnp.int32)
     to_scalars = pltpu.make_async_copy(ints, picks, sem)
     to_scalars.start()
+    lane = lax.broadcasted_iota(jnp.int32, rows.shape, 1)
+    return to_scalars, jnp.sum(jnp.where((lane & 31) == SLOTS, rows, 0.0))
+
+
+def add_islands(got, grid, picks):
+    group = lane_group((8, 128))
+
+    def some(a, carry):
+        for k in range(SHARE):
+            i = SHARE * a + k
+            tiles = [got[i, 0, 1024 * t:1024 * t + 1024].reshape(8, 128) for t in range(2)]
+            olds, news, masks, places = [], [], [], []
+            for j in range(SLOTS):
+                b = picks[a, 32 * k + j]
+                off = b & 7
+                place = b >> 3
+                news.append(pltpu.roll(tiles[j // 8], ((off - j % 8) & 7) * 16, 1))
+                olds.append(grid[place])
+                masks.append(group == off)
+                places.append(place)
+            for j in range(SLOTS):
+                pltpu.store(grid.at[places[j]], olds[j] + news[j], mask=masks[j])
+        return carry
+
+    lax.fori_loop(0, got.shape[0] // SHARE, some, 0)
+
+
+def scatter_kernel(got, factor, rest_m, rest_g, grid, steps, rest, ints, picks, rest_out, sem, out_sem):
+    to_scalars, total = gather_meta(got, ints, picks, sem)
+    steps[...] = jnp.full(steps.shape, total, F32)
     grid[...] = jnp.zeros_like(grid)
-    steps = jnp.sum(got[:, :, PAY + SLOTS:PAY + SLOTS + 1])
+    f = factor[:, :1]
+    cols = rest_out.shape[1]
+    width = cols // 4
+    copies = []
+    for q in range(4):
+        at = slice(width * q, width * q + width)
+        rest_out[:, at] = (rest_m[:, at] + f * rest_g[:, at]).astype(BF)
+        copies.append(pltpu.make_async_copy(rest_out.at[:, at], rest.at[:, at], out_sem.at[q]))
+        copies[q].start()
     to_scalars.wait()
-    group = lane_group((8, 128))
-
-    def one(i, carry):
-        tiles = [got[i, 0, 1024 * t:1024 * t + 1024].reshape(8, 128) for t in range(2)]
-        olds, news, masks, places = [], [], [], []
-        for j in range(SLOTS):
-            b = picks[i, 0, j]
-            off = b & 7
-            place = b >> 3
-            news.append(pltpu.roll(tiles[j // 8], ((off - j % 8) & 7) * 16, 1))
-            olds.append(grid[place])
-            masks.append(group == off)
-            places.append(place)
-        for j in range(SLOTS):
-            pltpu.store(grid.at[places[j]], olds[j] + news[j], mask=masks[j])
-        return carry
-
-    lax.fori_loop(0, got.shape[0], one, 0, unroll=4)
-    return steps
-
-
-def scatter_kernel(got, grid, steps, ints, picks, sem):
-    steps[...] = jnp.full(steps.shape, add_islands(got, grid, ints, picks, sem), F32)
-
-
-def scatter_call(got, rows, cols):
+    add_islands(got, grid, picks)
+    for c in copies:
+        c.wait()
+
+
+def scatter_call(got, factor, rest_m, rest_g):
+    rows, cols = rest_m.shape
     vm = pl.BlockSpec(memory_space=pltpu.VMEM)
     islands = got.shape[0]
     return pl.pallas_call(
         scatter_kernel,
-        in_specs=[vm],
-        out_specs=[vm, vm],
+        in_specs=[vm] * 4,
+        out_specs=[vm, vm, pl.BlockSpec(memory_space=pl.ANY)],
         out_shape=[
             jax.ShapeDtypeStruct((rows * cols // 1024, 8, 128), F32),
             jax.ShapeDtypeStruct((1, 128), F32),
+            jax.ShapeDtypeStruct((rows, cols), BF),
         ],
         scratch_shapes=[
-            pltpu.VMEM((islands, 1, 128), jnp.int32),
-            pltpu.SMEM((islands, 1, 128), jnp.int32),
+            pltpu.VMEM((islands // SHARE, 128), jnp.int32),
+            pltpu.SMEM((islands // SHARE, 128), jnp.int32),
+            pltpu.VMEM((rows, cols), BF),
             pltpu.SemaphoreType.DMA,
+            pltpu.SemaphoreType.DMA((4,)),
         ],
         compiler_params=pltpu.CompilerParams(vmem_limit_bytes=16 * MIB),
         cost_estimate=pl.CostEstimate(flops=300_000_000, bytes_accessed=8 * MIB, transcendentals=0),
         name="scatter_own",
-    )(got)
-
-
-def merge_kernel(got, first, first_steps, left3, wide_hi, wide_lo, out, grid, ints, picks, done, sem, out_sem):
-    islands = 2.0 * got.shape[0]
-    steps = add_islands(got, grid, ints, picks, sem)
-    s = islands / (steps + first_steps[0, 0])
+    )(got, factor, rest_m, rest_g)
+
+
+def merge_kernel(got, first, first_steps, left3, right2, out, grid, ints, picks, done, sem, out_sem):
+    to_scalars, total = gather_meta(got, ints, picks, sem)
+    grid[...] = jnp.zeros_like(grid)
+    s = 2.0 * got.shape[0] / (total + first_steps[0, 0])
+    to_scalars.wait()
+    add_islands(got, grid, picks)
     pairs = grid.shape[0] // 8
     width = 256 * GROUP
     copies = []
@@ -285,13 +318,13 @@
             parts.append(jnp.concatenate([grid[p] + first[p] for p in at], 0))
         hi, lo = split(jnp.concatenate(parts, 1))
         z = dot(left3[...], jnp.concatenate([hi, lo, hi], 0)) * s
-        z = jnp.concatenate([z[:, 256 * k:256 * k + 256] for k in range(GROUP)], 0)
+        z = jnp.concatenate([z[:, 128 * k:128 * k + 128] for k in range(2 * GROUP)], 0)
         hi, lo = split(z)
-        y = dot(hi, wide_hi[...]) + (dot(lo, wide_hi[...]) + dot(hi, wide_lo[...]))
-        y = y.astype(BF)
-        for k in range(GROUP):
-            at = 256 * (GROUP * q + k)
-            done[:, at:at + 256] = y[64 * k:64 * k + 64]
+        y = dot(jnp.concatenate([hi, lo], 1), right2[...])
+        y = (y[:, :128] + y[:, 128:]).astype(BF)
+        for k in range(2 * GROUP):
+            at = width * q + 128 * k
+            done[:, at:at + 128] = y[64 * k:64 * k + 64]
         at = slice(width * q, width * q + width)
         copies.append(pltpu.make_async_copy(done.at[:, at], out.at[:, at], out_sem.at[q]))
         copies[q].start()
@@ -305,13 +338,13 @@
     islands = got.shape[0]
     return pl.pallas_call(
         merge_kernel,
-        in_specs=[vm] * 6,
+        in_specs=[vm] * 5,
         out_specs=anyw,
         out_shape=jax.ShapeDtypeStruct((rows, cols), BF),
         scratch_shapes=[
             pltpu.VMEM((rows * cols // 1024, 8, 128), F32),
-            pltpu.VMEM((islands, 1, 128), jnp.int32),
-            pltpu.SMEM((islands, 1, 128), jnp.int32),
+            pltpu.VMEM((islands // SHARE, 128), jnp.int32),
+            pltpu.SMEM((islands // SHARE, 128), jnp.int32),
             pltpu.VMEM((rows, cols), BF),
             pltpu.SemaphoreType.DMA,
             pltpu.SemaphoreType.DMA((cols // (256 * GROUP),)),
@@ -319,7 +352,7 @@
         compiler_params=pltpu.CompilerParams(vmem_limit_bytes=32 * MIB),
         cost_estimate=pl.CostEstimate(flops=1_000_000_000, bytes_accessed=2 * MIB, transcendentals=0),
         name="merge_update",
-    )(got, first, first_steps, INV_LEFT3, INV_WIDE_HI, INV_WIDE_LO)
+    )(got, first, first_steps, INV_LEFT3, INV_RIGHT2)
 
 
 def on_device(weight, acts_t, out_grad, momentum, chosen, counts, steps):
@@ -331,30 +364,30 @@
     other_core = [(i, i ^ 1) for i in range(islands)]
     momentum = momentum[0]
 
-    picks = chosen[0] % (rows * cols // 128)
-    live = counts[0]
-
     grad, squares, og_held, weight_held = grad_call(acts_t, out_grad, weight)
+    grad, og_held, weight_held = [
+        pltpu.with_memory_space_constraint(x, pltpu.VMEM) for x in (grad, og_held, weight_held)
+    ]
     squares = squares + lax.ppermute(squares, "shard", [(i, i ^ 1) for i in range(shards)])
     acts_grad = acts_grad_call(weight_held, og_held)
     squares, acts_grad = lax.optimization_barrier((squares, acts_grad))
     squares = squares + lax.ppermute(squares, "shard", [(i, i ^ 3) for i in range(shards)])
-    coefs = coef_call(picks, live, momentum, grad)
-    squares, coefs = lax.optimization_barrier((squares, coefs))
+    picks = chosen[0] % (rows * cols // 128)
+    own_steps = steps.astype(F32)
+    meta = jnp.concatenate([picks.astype(F32), own_steps, jnp.zeros((111,), F32)])
+    coefs = coef_call(picks, counts[0], momentum, grad)
+    squares, coefs, meta = lax.optimization_barrier((squares, coefs, meta))
     pack_m, pack_g, rest_m, rest_g = coefs
 
-    mean = squares[0, :1] / float(rows * cols * shards)
+    mean = squares / float(rows * cols * shards)
     factor = jnp.minimum(1.0, 1.0 / jnp.sqrt(mean + 1e-06))
-    own_steps = steps.astype(F32)
     payload = (0.9 * pack_m + factor * pack_g) * own_steps
-    meta = jnp.concatenate([picks.astype(F32), own_steps, jnp.zeros((111,), F32)])
     sent = jnp.concatenate([payload.reshape(1, PAY), meta[None]], 1)
     sent = jnp.broadcast_to(sent[None], (half, 1, PAY + 128))
     got = lax.all_to_all(sent, "island", 0, 0, tiled=True, axis_index_groups=same_core)
     swapped = lax.ppermute(got, "island", other_core)
 
-    momentum_next = (rest_m + factor * rest_g).astype(BF)
-    first, first_steps = scatter_call(got, rows, cols)
+    first, first_steps, momentum_next = scatter_call(got, factor, rest_m, rest_g)
     update = merge_call(swapped, first, first_steps, rows, cols)
     return (update, momentum_next[None], acts_grad)
 

time: 48.6 us -> 46.4 us (0.955)
  other arithmetic: 1.3 us -> 0.15 us
  Pallas kernels: 15.3 us -> 14.3 us
    broadcast_in_dim x2 -> x0, other arithmetic: 1.24 us -> none  [the longest x1 1.16 us: on_device(): return (update, momentum_next[None], acts_grad)]
    pallas_call x2, Pallas kernels: 8.49 us -> 7.53 us  [the longest x1 4.71 us: merge_call(): pl.pallas_call(merge_kernel, in_specs=[vm] * 5, out_specs=anyw, out_shape...]
  transfers between devices with their start and end apart: 3 -> 3, of which waited for: 0 -> 0; matrix products, arithmetic and copies ran while one was open for 3% -> 0% of each run, Pallas kernels for 14% -> 15%
where the time goes in v3:
time: 46.4 us; the launch traced here: 46.3 us
  blocking collectives  21.5 us (46%)
  Pallas kernels  14.3 us (31%)
  starting transfers between devices  7.98 us (17%)
  between operations  2.11 us (5%)
    all_to_all x1, blocking collectives, on_device(): lax.all_to_all(sent, 'island', 0, 0, tiled=True, axis_index_groups=same_c...  21.5 us
    pallas_call x1, Pallas kernels, merge_call(): pl.pallas_call(merge_kernel, in_specs=[vm] * 5, out_specs=anyw, out_shape...  4.71 us
    ppermute x1, starting transfers between devices, on_device(): swapped = lax.ppermute(got, 'island', other_core)  3.95 us
    pallas_call x1, Pallas kernels, grad_call(): pl.pallas_call(grad_kernel, in_specs=[anyw] * 3, out_specs=[vm] * 4, out_...  2.89 us
    pallas_call x1, Pallas kernels, scatter_call(): pl.pallas_call(scatter_kernel, in_specs=[vm] * 4, out_specs=[vm, vm, pl.B...  2.82 us
    ppermute x1, starting transfers between devices, on_device(): lax.ppermute(squares, 'shard', [(i, i ^ 1) for i in range(shards)])  2.13 us
    pallas_call x1, Pallas kernels, coef_call(): pl.pallas_call(coef_kernel, in_specs=[sm, sm] + [vm] * 7, out_specs=[vm]...  1.99 us
    ppermute x1, starting transfers between devices, on_device(): lax.ppermute(squares, 'shard', [(i, i ^ 3) for i in range(shards)])  1.9 us
  transfers between devices with their start and end apart: 3, of which 0 were waited for; matrix products, arithmetic and copies ran while one was open for 0% of the time, Pallas kernels for 15%

profile of v3, /device:TPU:1, one launch (start us, length us, event | category | flops | bytes accessed | tf_op | source)
XLA Modules:
  0.0 46.3 jit_solution(2160994075129460805)
XLA Ops:
  0.6 0.0 copy-start.7
  0.6 2.9 %weight_grad.1 = (f32[64,8192]{1,0:T(8,128)S(1)}, f32[1,128]{1,0:T(1,128)S(1)}, bf16[256,8192]{1,0:T(8,128)(2,1)S(1)}, bf16[64,8192]{1,0:T(8,128)(2,1)S(1)}) custom-call(bf16[64,256]{1,0:T(8,128)(2,1)} %acts.1, bf16[256,8192]{1,0:T(8,128)(2,1)} %og.1, bf16[64,8192]{1,0:T(8,128)(2,1)} %weight.1), custom_call_target="tpu_custom_call" | custom-call | flops 268435456 | bytes 6291456 | tf_op jit(solution)/shard_map/weight_grad/pallas_call | solution.py:97
  3.5 2.1 %collective-permute-start = (f32[1,128]{1,0:T(1,128)S(1)}, f32[1,128]{1,0:T(1,128)S(1)}, u32[]{:S(2)}, u32[]{:S(2)}) collective-permute-start(f32[1,128]{1,0:T(1,128)S(1)} %get-tuple-element.22), channel_id=1, source_target_pairs={{0,1},{1,0},{2,3},{3,2},{4,5},{5,4},{6,7},{7,6},{8,9},{9,8},{10,11... | collective-permute-start | bytes 1544 | tf_op jit(solution)/shard_map/ppermute | solution.py:371
  6.3 0.0 copy-done.7
  6.4 0.1 pad_maximum_fusion
  6.4 0.0 copy-start
  6.4 0.0 copy-start.1
  6.4 0.0 copy-start.2
  6.4 0.0 copy-start.3
  6.4 0.0 copy-start.4
  6.5 0.0 copy-start.5
  6.5 1.9 %acts_grad.1 = bf16[64,256]{1,0:T(8,128)(2,1)} custom-call(bf16[64,8192]{1,0:T(8,128)(2,1)S(1)} %get-tuple-element.23.weight, bf16[256,8192]{1,0:T(8,128)(2,1)S(1)} %get-tuple-element.24.og), custom_call_target="tpu_custom_call" | custom-call | flops 268435456 | bytes 5242880 | tf_op jit(solution)/shard_map/acts_grad/pallas_call | solution.py:126
  9.0 0.0 collective-permute-done
  9.0 1.9 %collective-permute-start.1 = (f32[1,128]{1,0:T(1,128)S(1)}, f32[1,128]{1,0:T(1,128)S(1)}, u32[]{:S(2)}, u32[]{:S(2)}) collective-permute-start(f32[1,128]{1,0:T(1,128)S(1)} %add.21), channel_id=1, source_target_pairs={{0,3},{1,2},{2,1},{3,0},{4,7},{5,6},{6,5},{7,4},{8,11},{9,10},{10,... | collective-permute-start | bytes 1544 | tf_op jit(solution)/shard_map/ppermute | solution.py:374
  10.9 0.0 copy-done
  11.0 0.0 copy-done.1
  11.0 0.0 copy-done.2
  11.0 0.0 copy-done.3
  11.0 0.0 copy-done.4
  11.0 0.0 copy-done.5
  11.0 2.0 %selected_coefs.1 = (f32[16,128]{1,0:T(8,128)S(1)}, f32[16,128]{1,0:T(8,128)S(1)}, f32[64,8192]{1,0:T(8,128)S(1)}, f32[64,8192]{1,0:T(8,128)S(1)}) custom-call(s32[16]{0:T(128)S(1)} %get-tuple-element.42.picks, s32[1]{0:T(128)} %bitcast.11.counts, bf16[64,8192]{1,0:T(8,128)(2,1)S(1)} %bitcast.12, f32[64,8192]{1,0:T(8,128)S(1)} %get-tuple-element.26.grad, ...), custom_call_target="tpu_custom_call" | custom-call | flops 300000000 | bytes 8388608 | tf_op jit(solution)/shard_map/selected_coefs/pallas_call | solution.py:195
  13.0 0.0 collective-permute-done.1
  13.1 0.1 broadcast_in_dim.21
  13.2 21.5 %all_to_all.5.got = f32[32,1,2176]{2,1,0:T(1,128)S(1)} all-to-all(f32[32,1,2176]{2,1,0:T(1,128)S(1)} %broadcast_in_dim.21), channel_id=1, replica_groups={{0,8,16,24,32,40,48,56,64,72,80,88,96,104,112,120,128,136,144,152,160,1..., dimensions={0} | all-to-all | bytes 557056 | tf_op jit(solution)/shard_map/all_to_all | solution.py:387
  34.8 3.9 %collective-permute-start.2 = (f32[32,1,2176]{2,1,0:T(1,128)S(1)}, f32[32,1,2176]{2,1,0:T(1,128)S(1)}, u32[]{:S(2)}, u32[]{:S(2)}) collective-permute-start(f32[32,1,2176]{2,1,0:T(1,128)S(1)} %all_to_all.5.got), channel_id=1, source_target_pairs={{0,4},{4,0},{8,12},{12,8},{16,20},{20,16},{24,28},{28,24},{32,36},... | collective-permute-start | bytes 835592 | tf_op jit(solution)/shard_map/ppermute | solution.py:388
  38.7 0.0 copy-start.6
  38.7 2.8 %scatter_own.1 = (f32[512,8,128]{2,1,0:T(8,128)S(1)}, f32[1,128]{1,0:T(1,128)S(1)}, bf16[64,8192]{1,0:T(8,128)(2,1)}) custom-call(f32[32,1,2176]{2,1,0:T(1,128)S(1)} %all_to_all.5.got, f32[1,128]{1,0:T(1,128)S(1)} %rsqrt_minimum_fusion.factor, f32[64,8192]{1,0:T(8,128)S(1)} %get-tuple-element.35.rest_m, f32[64,8192]{1,0:T(8,128)S(1)} %get-tuple-element.36.rest_g), custom_call_target="tpu_custom_call" | custom-call | flops 300000000 | bytes 8388608 | tf_op jit(solution)/shard_map/scatter_own/pallas_call | solution.py:283
  41.6 0.0 collective-permute-done.2.got
  41.6 0.0 copy-done.6
  41.6 4.7 %merge_update.1 = bf16[64,8192]{1,0:T(8,128)(2,1)} custom-call(f32[32,1,2176]{2,1,0:T(1,128)S(1)} %collective-permute-done.2.got, f32[512,8,128]{2,1,0:T(8,128)S(1)} %get-tuple-element.37.first, f32[1,128]{1,0:T(1,128)S(1)} %get-tuple-element.38.first_steps, bf16[64,192]{1,0:T(8,128)(2,1)S(1)} %copy-done.3, bf16[256,256]{1,0:T(8,128)(2,1)S(1)} %copy-done.6), custom_call_target="tpu_custom_call" | custom-call | flops 1000000000 | bytes 2097152 | tf_op jit(solution)/shard_map/merge_update/pallas_call | solution.py:339
  (8 shorter events, 0.1 us)
Async XLA Ops:
  0.6 5.7 %copy-start.7 = (s32[1,16]{1,0:T(1,128)S(1)}, s32[1,16]{1,0:T(1,128)}, u32[]{:S(2)}) copy-start(s32[1,16]{1,0:T(1,128)} %param.17) | copy-start | bytes 196
  3.5 5.5 %collective-permute-start = (f32[1,128]{1,0:T(1,128)S(1)}, f32[1,128]{1,0:T(1,128)S(1)}, u32[]{:S(2)}, u32[]{:S(2)}) collective-permute-start(f32[1,128]{1,0:T(1,128)S(1)} %get-tuple-element.22), channel_id=1, source_target_pairs={{0,1},{1,0},{2,3},{3,2},{4,5},{5,4},{6,7},{7,6},{8,9},{9,8},{10,11... | collective-permute-start | bytes 1544 | tf_op jit(solution)/shard_map/ppermute | solution.py:371
  6.4 4.5 %copy-start = (bf16[1,64,8192]{2,1,0:T(8,128)(2,1)S(1)}, bf16[1,64,8192]{2,1,0:T(8,128)(2,1)}, u32[]{:S(2)}) copy-start(bf16[1,64,8192]{2,1,0:T(8,128)(2,1)} %param.16) | copy-start | bytes 3145732
  6.4 4.5 %copy-start.1 = (bf16[384,128]{1,0:T(8,128)(2,1)S(1)}, bf16[384,128]{1,0:T(8,128)(2,1)}, u32[]{:S(2)}) copy-start(bf16[384,128]{1,0:T(8,128)(2,1)} %constant.42.clone.back_right3) | copy-start | bytes 294916
  6.4 4.5 %copy-start.2 = (bf16[384,128]{1,0:T(8,128)(2,1)S(1)}, bf16[384,128]{1,0:T(8,128)(2,1)}, u32[]{:S(2)}) copy-start(bf16[384,128]{1,0:T(8,128)(2,1)} %constant.40.clone.right3) | copy-start | bytes 294916
  6.4 4.5 %copy-start.3 = (bf16[64,192]{1,0:T(8,128)(2,1)S(1)}, bf16[64,192]{1,0:T(8,128)(2,1)}, u32[]{:S(2)}) copy-start(bf16[64,192]{1,0:T(8,128)(2,1)} %constant.41.clone.back_left3.left3) | copy-start | bytes 73732
  6.4 4.5 %copy-start.4 = (bf16[64,192]{1,0:T(8,128)(2,1)S(1)}, bf16[64,192]{1,0:T(8,128)(2,1)}, u32[]{:S(2)}) copy-start(bf16[64,192]{1,0:T(8,128)(2,1)} %constant.39.clone.left3) | copy-start | bytes 73732
  6.5 4.5 %copy-start.5 = (bf16[64,128]{1,0:T(8,128)(2,1)S(1)}, bf16[64,128]{1,0:T(8,128)(2,1)}, u32[]{:S(2)}) copy-start(bf16[64,128]{1,0:T(8,128)(2,1)} %constant.38.clone.left2) | copy-start | bytes 49156
  9.0 3.9 %collective-permute-start.1 = (f32[1,128]{1,0:T(1,128)S(1)}, f32[1,128]{1,0:T(1,128)S(1)}, u32[]{:S(2)}, u32[]{:S(2)}) collective-permute-start(f32[1,128]{1,0:T(1,128)S(1)} %add.21), channel_id=1, source_target_pairs={{0,3},{1,2},{2,1},{3,0},{4,7},{5,6},{6,5},{7,4},{8,11},{9,10},{10,... | collective-permute-start | bytes 1544 | tf_op jit(solution)/shard_map/ppermute | solution.py:374
  34.8 6.8 %collective-permute-start.2 = (f32[32,1,2176]{2,1,0:T(1,128)S(1)}, f32[32,1,2176]{2,1,0:T(1,128)S(1)}, u32[]{:S(2)}, u32[]{:S(2)}) collective-permute-start(f32[32,1,2176]{2,1,0:T(1,128)S(1)} %all_to_all.5.got), channel_id=1, source_target_pairs={{0,4},{4,0},{8,12},{12,8},{16,20},{20,16},{24,28},{28,24},{32,36},... | collective-permute-start | bytes 835592 | tf_op jit(solution)/shard_map/ppermute | solution.py:388
  38.7 2.8 %copy-start.6 = (bf16[256,256]{1,0:T(8,128)(2,1)S(1)}, bf16[256,256]{1,0:T(8,128)(2,1)}, u32[]{:S(2)}) copy-start(bf16[256,256]{1,0:T(8,128)(2,1)} %constant.43.clone.right2) | copy-start | bytes 393220

commit v4 on v3

--- a/solution.py
+++ b/solution.py
@@ -41,6 +41,8 @@
 FWD_LEFT3 = np.concatenate([COS_HI, COS_HI, COS_LO], 1)
 FWD_LEFT2 = np.concatenate([COS_HI, COS_LO], 1)
 INV_LEFT3 = np.concatenate([INV_HI, INV_HI, INV_LO], 1)
+MIRROR = np.array([8 * r + (8 - u) % 8 for r in range(8) for u in range(8)])
+INV_LEFT3_MIRROR = np.concatenate([INV_HI[:, MIRROR], INV_HI[:, MIRROR], INV_LO[:, MIRROR]], 1)
 FWD_RIGHT3 = np.concatenate([diagonal(COS_HI.T, 2), diagonal(COS_HI.T, 2), diagonal(COS_LO.T, 2)], 0)
 INV_RIGHT3 = np.concatenate([diagonal(COS_HI, 2), diagonal(COS_HI, 2), diagonal(COS_LO, 2)], 0)
 INV_RIGHT2 = np.block([
@@ -163,14 +165,12 @@
     live = counts[0]
     wants = [jnp.where(j < live, offs[j], 8) for j in range(SLOTS)]
     for base, pack in ((0, pack_m), (128, pack_g)):
-        packed = [jnp.zeros((8, 128), F32)] * 2
         for j in range(SLOTS):
             at = slice(base + 8 * j, base + 8 * j + 8)
             kept = jnp.where(group == wants[j], low[at, :], 0.0)
             low[at, :] = kept
-            packed[j // 8] = packed[j // 8] + pltpu.roll(kept, ((j % 8 - offs[j]) & 7) * 16, 1)
-        pack[0:8, :] = packed[0]
-        pack[8:16, :] = packed[1]
+            turned = pltpu.roll(kept, 0, 1, stride=16, stride_axis=0)
+            pack[j:j + 1, :] = jnp.sum(turned, axis=0, keepdims=True)
     hi, lo = split(low[...])
     low[...] = dot(jnp.concatenate([hi, lo, hi], 1), back_right3[...])
     for j in range(SLOTS):
@@ -235,26 +235,22 @@
 
 
 def add_islands(got, grid, picks):
-    group = lane_group((8, 128))
-
     def some(a, carry):
         for k in range(SHARE):
             i = SHARE * a + k
-            tiles = [got[i, 0, 1024 * t:1024 * t + 1024].reshape(8, 128) for t in range(2)]
-            olds, news, masks, places = [], [], [], []
+            places = [pl.ds(pl.multiple_of(picks[a, 32 * k + j] * 128, 128), 128) for j in range(SLOTS)]
+            sums = [grid[0, places[j]] + got[i, 0, 128 * j:128 * j + 128] for j in range(SLOTS)]
             for j in range(SLOTS):
-                b = picks[a, 32 * k + j]
-                off = b & 7
-                place = b >> 3
-                news.append(pltpu.roll(tiles[j // 8], ((off - j % 8) & 7) * 16, 1))
-                olds.append(grid[place])
-                masks.append(group == off)
-                places.append(place)
-            for j in range(SLOTS):
-                pltpu.store(grid.at[places[j]], olds[j] + news[j], mask=masks[j])
+                grid[0, places[j]] = sums[j]
         return carry
 
     lax.fori_loop(0, got.shape[0] // SHARE, some, 0)
+
+
+def untwist(x, group):
+    for k in range(3):
+        x = jnp.where((group & (1 << k)) != 0, pltpu.roll(x, 8 - (1 << k), 0), x)
+    return pltpu.roll(x, 0, 1, stride=16, stride_axis=0)
 
 
 def scatter_kernel(got, factor, rest_m, rest_g, grid, steps, rest, ints, picks, rest_out, sem, out_sem):
@@ -285,7 +281,7 @@
         in_specs=[vm] * 4,
         out_specs=[vm, vm, pl.BlockSpec(memory_space=pl.ANY)],
         out_shape=[
-            jax.ShapeDtypeStruct((rows * cols // 1024, 8, 128), F32),
+            jax.ShapeDtypeStruct((1, rows * cols), F32),
             jax.ShapeDtypeStruct((1, 128), F32),
             jax.ShapeDtypeStruct((rows, cols), BF),
         ],
@@ -308,14 +304,19 @@
     s = 2.0 * got.shape[0] / (total + first_steps[0, 0])
     to_scalars.wait()
     add_islands(got, grid, picks)
-    pairs = grid.shape[0] // 8
+    pairs = grid.shape[1] // 8192
     width = 256 * GROUP
+    group = lane_group((8, 128))
     copies = []
     for q in range(pairs // (2 * GROUP)):
         parts = []
         for k in range(2 * GROUP):
-            at = [r * pairs + 2 * GROUP * q + k for r in range(8)]
-            parts.append(jnp.concatenate([grid[p] + first[p] for p in at], 0))
+            tiles = []
+            for r in range(8):
+                at = 1024 * (r * pairs + 2 * GROUP * q + k)
+                tile = (grid[0, at:at + 1024] + first[0, at:at + 1024]).reshape(8, 128)
+                tiles.append(untwist(tile, group))
+            parts.append(jnp.concatenate(tiles, 0))
         hi, lo = split(jnp.concatenate(parts, 1))
         z = dot(left3[...], jnp.concatenate([hi, lo, hi], 0)) * s
         z = jnp.concatenate([z[:, 128 * k:128 * k + 128] for k in range(2 * GROUP)], 0)
@@ -342,7 +343,7 @@
         out_specs=anyw,
         out_shape=jax.ShapeDtypeStruct((rows, cols), BF),
         scratch_shapes=[
-            pltpu.VMEM((rows * cols // 1024, 8, 128), F32),
+            pltpu.VMEM((1, rows * cols), F32),
             pltpu.VMEM((islands // SHARE, 128), jnp.int32),
             pltpu.SMEM((islands // SHARE, 128), jnp.int32),
             pltpu.VMEM((rows, cols), BF),
@@ -352,7 +353,7 @@
         compiler_params=pltpu.CompilerParams(vmem_limit_bytes=32 * MIB),
         cost_estimate=pl.CostEstimate(flops=1_000_000_000, bytes_accessed=2 * MIB, transcendentals=0),
         name="merge_update",
-    )(got, first, first_steps, INV_LEFT3, INV_RIGHT2)
+    )(got, first, first_steps, INV_LEFT3_MIRROR, INV_RIGHT2)
 
 
 def on_device(weight, acts_t, out_grad, momentum, chosen, counts, steps):

time: 46.4 us -> 44.4 us (0.957)
  Pallas kernels: 14.3 us -> 12.2 us
    pallas_call x1, Pallas kernels: 2.82 us -> 1.65 us  [scatter_call(): pl.pallas_call(scatter_kernel, in_specs=[vm] * 4, out_specs=[vm, vm, pl.B...]
    pallas_call x1, Pallas kernels: 4.71 us -> 3.78 us  [merge_call(): pl.pallas_call(merge_kernel, in_specs=[vm] * 5, out_specs=anyw, out_shape...]
  transfers between devices with their start and end apart: 3 -> 3, of which waited for: 0 -> 0; matrix products, arithmetic and copies ran while one was open for 0% -> 0% of each run, Pallas kernels for 15% -> 13%
where the time goes in v4:
time: 44.4 us; the launch traced here: 44.2 us
  blocking collectives  21.5 us (48%)
  Pallas kernels  12.2 us (27%)
  starting transfers between devices  7.98 us (18%)
  between operations  2.12 us (5%)
    all_to_all x1, blocking collectives, on_device(): lax.all_to_all(sent, 'island', 0, 0, tiled=True, axis_index_groups=same_c...  21.5 us
    ppermute x1, starting transfers between devices, on_device(): swapped = lax.ppermute(got, 'island', other_core)  3.95 us
    pallas_call x1, Pallas kernels, merge_call(): pl.pallas_call(merge_kernel, in_specs=[vm] * 5, out_specs=anyw, out_shape...  3.78 us
    pallas_call x1, Pallas kernels, grad_call(): pl.pallas_call(grad_kernel, in_specs=[anyw] * 3, out_specs=[vm] * 4, out_...  2.89 us
    ppermute x1, starting transfers between devices, on_device(): lax.ppermute(squares, 'shard', [(i, i ^ 1) for i in range(shards)])  2.13 us
    pallas_call x1, Pallas kernels, coef_call(): pl.pallas_call(coef_kernel, in_specs=[sm, sm] + [vm] * 7, out_specs=[vm]...  2 us
    ppermute x1, starting transfers between devices, on_device(): lax.ppermute(squares, 'shard', [(i, i ^ 3) for i in range(shards)])  1.9 us
    pallas_call x1, Pallas kernels, acts_grad_call(): pl.pallas_call(acts_grad_kernel, in_specs=[vm, vm], out_specs=vm, out_sha...  1.9 us
  transfers between devices with their start and end apart: 3, of which 0 were waited for; matrix products, arithmetic and copies ran while one was open for 0% of the time, Pallas kernels for 13%

profile of v4, /device:TPU:1, one launch (start us, length us, event | category | flops | bytes accessed | tf_op | source)
XLA Modules:
  0.0 44.2 jit_solution(12276221504438108745)
XLA Ops:
  0.6 0.0 copy-start.8
  0.6 2.9 %weight_grad.1 = (f32[64,8192]{1,0:T(8,128)S(1)}, f32[1,128]{1,0:T(1,128)S(1)}, bf16[256,8192]{1,0:T(8,128)(2,1)S(1)}, bf16[64,8192]{1,0:T(8,128)(2,1)S(1)}) custom-call(bf16[64,256]{1,0:T(8,128)(2,1)} %acts.1, bf16[256,8192]{1,0:T(8,128)(2,1)} %og.1, bf16[64,8192]{1,0:T(8,128)(2,1)} %weight.1), custom_call_target="tpu_custom_call" | custom-call | flops 268435456 | bytes 6291456 | tf_op jit(solution)/shard_map/weight_grad/pallas_call | solution.py:99
  3.5 2.1 %collective-permute-start = (f32[1,128]{1,0:T(1,128)S(1)}, f32[1,128]{1,0:T(1,128)S(1)}, u32[]{:S(2)}, u32[]{:S(2)}) collective-permute-start(f32[1,128]{1,0:T(1,128)S(1)} %get-tuple-element.22), channel_id=1, source_target_pairs={{0,1},{1,0},{2,3},{3,2},{4,5},{5,4},{6,7},{7,6},{8,9},{9,8},{10,11... | collective-permute-start | bytes 1544 | tf_op jit(solution)/shard_map/ppermute | solution.py:372
  6.3 0.0 copy-done.8
  6.4 0.1 pad_maximum_fusion
  6.4 0.0 copy-start
  6.4 0.0 copy-start.1
  6.4 0.0 copy-start.2
  6.4 0.0 copy-start.3
  6.4 0.0 copy-start.4
  6.5 0.0 copy-start.5
  6.5 1.9 %acts_grad.1 = bf16[64,256]{1,0:T(8,128)(2,1)} custom-call(bf16[64,8192]{1,0:T(8,128)(2,1)S(1)} %get-tuple-element.23.weight, bf16[256,8192]{1,0:T(8,128)(2,1)S(1)} %get-tuple-element.24.og), custom_call_target="tpu_custom_call" | custom-call | flops 268435456 | bytes 5242880 | tf_op jit(solution)/shard_map/acts_grad/pallas_call | solution.py:128
  9.0 0.0 collective-permute-done
  9.0 1.9 %collective-permute-start.1 = (f32[1,128]{1,0:T(1,128)S(1)}, f32[1,128]{1,0:T(1,128)S(1)}, u32[]{:S(2)}, u32[]{:S(2)}) collective-permute-start(f32[1,128]{1,0:T(1,128)S(1)} %add.21), channel_id=1, source_target_pairs={{0,3},{1,2},{2,1},{3,0},{4,7},{5,6},{6,5},{7,4},{8,11},{9,10},{10,... | collective-permute-start | bytes 1544 | tf_op jit(solution)/shard_map/ppermute | solution.py:375
  10.9 0.0 copy-done
  11.0 0.0 copy-done.1
  11.0 0.0 copy-done.2
  11.0 0.0 copy-done.3
  11.0 0.0 copy-done.4
  11.0 0.0 copy-done.5
  11.0 2.0 %selected_coefs.1 = (f32[16,128]{1,0:T(8,128)S(1)}, f32[16,128]{1,0:T(8,128)S(1)}, f32[64,8192]{1,0:T(8,128)S(1)}, f32[64,8192]{1,0:T(8,128)S(1)}) custom-call(s32[16]{0:T(128)S(1)} %get-tuple-element.42.picks, s32[1]{0:T(128)} %bitcast.11.counts, bf16[64,8192]{1,0:T(8,128)(2,1)S(1)} %bitcast.12, f32[64,8192]{1,0:T(8,128)S(1)} %get-tuple-element.26.grad, ...), custom_call_target="tpu_custom_call" | custom-call | flops 300000000 | bytes 8388608 | tf_op jit(solution)/shard_map/selected_coefs/pallas_call | solution.py:195
  13.0 0.0 collective-permute-done.1
  13.1 0.1 broadcast_in_dim.21
  13.2 21.5 %all_to_all.5.got = f32[32,1,2176]{2,1,0:T(1,128)S(1)} all-to-all(f32[32,1,2176]{2,1,0:T(1,128)S(1)} %broadcast_in_dim.21), channel_id=1, replica_groups={{0,8,16,24,32,40,48,56,64,72,80,88,96,104,112,120,128,136,144,152,160,1..., dimensions={0} | all-to-all | bytes 557056 | tf_op jit(solution)/shard_map/all_to_all | solution.py:388
  34.8 3.9 %collective-permute-start.2 = (f32[32,1,2176]{2,1,0:T(1,128)S(1)}, f32[32,1,2176]{2,1,0:T(1,128)S(1)}, u32[]{:S(2)}, u32[]{:S(2)}) collective-permute-start(f32[32,1,2176]{2,1,0:T(1,128)S(1)} %all_to_all.5.got), channel_id=1, source_target_pairs={{0,4},{4,0},{8,12},{12,8},{16,20},{20,16},{24,28},{28,24},{32,36},... | collective-permute-start | bytes 835592 | tf_op jit(solution)/shard_map/ppermute | solution.py:389
  38.7 0.0 copy-start.6
  38.7 0.0 copy-start.7
  38.7 1.7 %scatter_own.1 = (f32[1,524288]{1,0:T(1,128)S(1)}, f32[1,128]{1,0:T(1,128)S(1)}, bf16[64,8192]{1,0:T(8,128)(2,1)}) custom-call(f32[32,1,2176]{2,1,0:T(1,128)S(1)} %all_to_all.5.got, f32[1,128]{1,0:T(1,128)S(1)} %rsqrt_minimum_fusion.factor, f32[64,8192]{1,0:T(8,128)S(1)} %get-tuple-element.35.rest_m, f32[64,8192]{1,0:T(8,128)S(1)} %get-tuple-element.36.rest_g), custom_call_target="tpu_custom_call" | custom-call | flops 300000000 | bytes 8388608 | tf_op jit(solution)/shard_map/scatter_own/pallas_call | solution.py:279
  40.4 0.0 collective-permute-done.2.got
  40.4 0.0 copy-done.6
  40.4 0.0 copy-done.7
  40.4 3.8 %merge_update.1 = bf16[64,8192]{1,0:T(8,128)(2,1)} custom-call(f32[32,1,2176]{2,1,0:T(1,128)S(1)} %collective-permute-done.2.got, f32[1,524288]{1,0:T(1,128)S(1)} %get-tuple-element.37.first, f32[1,128]{1,0:T(1,128)S(1)} %get-tuple-element.38.first_steps, bf16[64,192]{1,0:T(8,128)(2,1)S(1)} %copy-done.7, bf16[256,256]{1,0:T(8,128)(2,1)S(1)} %copy-done.6), custom_call_target="tpu_custom_call" | custom-call | flops 1000000000 | bytes 2097152 | tf_op jit(solution)/shard_map/merge_update/pallas_call | solution.py:340
  (8 shorter events, 0.1 us)
Async XLA Ops:
  0.6 5.7 %copy-start.8 = (s32[1,16]{1,0:T(1,128)S(1)}, s32[1,16]{1,0:T(1,128)}, u32[]{:S(2)}) copy-start(s32[1,16]{1,0:T(1,128)} %param.18) | copy-start | bytes 196
  3.5 5.5 %collective-permute-start = (f32[1,128]{1,0:T(1,128)S(1)}, f32[1,128]{1,0:T(1,128)S(1)}, u32[]{:S(2)}, u32[]{:S(2)}) collective-permute-start(f32[1,128]{1,0:T(1,128)S(1)} %get-tuple-element.22), channel_id=1, source_target_pairs={{0,1},{1,0},{2,3},{3,2},{4,5},{5,4},{6,7},{7,6},{8,9},{9,8},{10,11... | collective-permute-start | bytes 1544 | tf_op jit(solution)/shard_map/ppermute | solution.py:372
  6.4 4.5 %copy-start = (bf16[1,64,8192]{2,1,0:T(8,128)(2,1)S(1)}, bf16[1,64,8192]{2,1,0:T(8,128)(2,1)}, u32[]{:S(2)}) copy-start(bf16[1,64,8192]{2,1,0:T(8,128)(2,1)} %param.17) | copy-start | bytes 3145732
  6.4 4.5 %copy-start.1 = (bf16[384,128]{1,0:T(8,128)(2,1)S(1)}, bf16[384,128]{1,0:T(8,128)(2,1)}, u32[]{:S(2)}) copy-start(bf16[384,128]{1,0:T(8,128)(2,1)} %constant.44.clone.back_right3) | copy-start | bytes 294916
  6.4 4.5 %copy-start.2 = (bf16[384,128]{1,0:T(8,128)(2,1)S(1)}, bf16[384,128]{1,0:T(8,128)(2,1)}, u32[]{:S(2)}) copy-start(bf16[384,128]{1,0:T(8,128)(2,1)} %constant.42.clone.right3) | copy-start | bytes 294916
  6.4 4.5 %copy-start.3 = (bf16[64,192]{1,0:T(8,128)(2,1)S(1)}, bf16[64,192]{1,0:T(8,128)(2,1)}, u32[]{:S(2)}) copy-start(bf16[64,192]{1,0:T(8,128)(2,1)} %constant.43.clone.back_left3) | copy-start | bytes 73732
  6.4 4.5 %copy-start.4 = (bf16[64,192]{1,0:T(8,128)(2,1)S(1)}, bf16[64,192]{1,0:T(8,128)(2,1)}, u32[]{:S(2)}) copy-start(bf16[64,192]{1,0:T(8,128)(2,1)} %constant.41.clone.left3) | copy-start | bytes 73732
  6.5 4.5 %copy-start.5 = (bf16[64,128]{1,0:T(8,128)(2,1)S(1)}, bf16[64,128]{1,0:T(8,128)(2,1)}, u32[]{:S(2)}) copy-start(bf16[64,128]{1,0:T(8,128)(2,1)} %constant.40.clone.left2) | copy-start | bytes 49156
  9.0 3.9 %collective-permute-start.1 = (f32[1,128]{1,0:T(1,128)S(1)}, f32[1,128]{1,0:T(1,128)S(1)}, u32[]{:S(2)}, u32[]{:S(2)}) collective-permute-start(f32[1,128]{1,0:T(1,128)S(1)} %add.21), channel_id=1, source_target_pairs={{0,3},{1,2},{2,1},{3,0},{4,7},{5,6},{6,5},{7,4},{8,11},{9,10},{10,... | collective-permute-start | bytes 1544 | tf_op jit(solution)/shard_map/ppermute | solution.py:375
  34.8 5.6 %collective-permute-start.2 = (f32[32,1,2176]{2,1,0:T(1,128)S(1)}, f32[32,1,2176]{2,1,0:T(1,128)S(1)}, u32[]{:S(2)}, u32[]{:S(2)}) collective-permute-start(f32[32,1,2176]{2,1,0:T(1,128)S(1)} %all_to_all.5.got), channel_id=1, source_target_pairs={{0,4},{4,0},{8,12},{12,8},{16,20},{20,16},{24,28},{28,24},{32,36},... | collective-permute-start | bytes 835592 | tf_op jit(solution)/shard_map/ppermute | solution.py:389
  38.7 1.7 %copy-start.6 = (bf16[256,256]{1,0:T(8,128)(2,1)S(1)}, bf16[256,256]{1,0:T(8,128)(2,1)}, u32[]{:S(2)}) copy-start(bf16[256,256]{1,0:T(8,128)(2,1)} %constant.46.clone.right2) | copy-start | bytes 393220
  38.7 1.7 %copy-start.7 = (bf16[64,192]{1,0:T(8,128)(2,1)S(1)}, bf16[64,192]{1,0:T(8,128)(2,1)}, u32[]{:S(2)}) copy-start(bf16[64,192]{1,0:T(8,128)(2,1)} %constant.45.clone.left3) | copy-start | bytes 73732

commit v5 on v4

--- a/solution.py
+++ b/solution.py
@@ -116,9 +116,19 @@
     )(*held)
 
 
+def last_half():
+    return lax.axis_index("island") >= lax.axis_size("island") // 2
+
+
+def acts_product(weight, og):
+    total = lax.dot_general(og, weight, (((1,), (1,)), ((), ())), preferred_element_type=F32)
+    return total.T.astype(BF)
+
+
 def acts_grad_kernel(weight, og, out):
-    total = lax.dot_general(og[...], weight[...], (((1,), (1,)), ((), ())), preferred_element_type=F32)
-    out[...] = total.T.astype(BF)
+    @pl.when(jnp.logical_not(last_half()))
+    def _():
+        out[...] = acts_product(weight[...], og[...])
 
 
 def acts_grad_call(weight, og):
@@ -244,7 +254,7 @@
                 grid[0, places[j]] = sums[j]
         return carry
 
-    lax.fori_loop(0, got.shape[0] // SHARE, some, 0)
+    lax.fori_loop(0, got.shape[0] // SHARE, some, 0, unroll=4)
 
 
 def untwist(x, group):
@@ -298,9 +308,21 @@
     )(got, factor, rest_m, rest_g)
 
 
-def merge_kernel(got, first, first_steps, left3, right2, out, grid, ints, picks, done, sem, out_sem):
+def merge_kernel(got, first, first_steps, left3, right2, weight, og, acts_early, out, acts_out,
+                 grid, ints, picks, done, weight_in, og_in, acts_in, sem, out_sem, acts_sem):
+    late = last_half()
+    fetch = [
+        pltpu.make_async_copy(weight, weight_in, acts_sem.at[0]),
+        pltpu.make_async_copy(og, og_in, acts_sem.at[1]),
+    ]
+
+    @pl.when(late)
+    def _():
+        for c in fetch:
+            c.start()
+
     to_scalars, total = gather_meta(got, ints, picks, sem)
-    grid[...] = jnp.zeros_like(grid)
+    grid[...] = first[...]
     s = 2.0 * got.shape[0] / (total + first_steps[0, 0])
     to_scalars.wait()
     add_islands(got, grid, picks)
@@ -314,8 +336,7 @@
             tiles = []
             for r in range(8):
                 at = 1024 * (r * pairs + 2 * GROUP * q + k)
-                tile = (grid[0, at:at + 1024] + first[0, at:at + 1024]).reshape(8, 128)
-                tiles.append(untwist(tile, group))
+                tiles.append(untwist(grid[0, at:at + 1024].reshape(8, 128), group))
             parts.append(jnp.concatenate(tiles, 0))
         hi, lo = split(jnp.concatenate(parts, 1))
         z = dot(left3[...], jnp.concatenate([hi, lo, hi], 0)) * s
@@ -329,31 +350,54 @@
         at = slice(width * q, width * q + width)
         copies.append(pltpu.make_async_copy(done.at[:, at], out.at[:, at], out_sem.at[q]))
         copies[q].start()
+
+    @pl.when(late)
+    def _():
+        for c in fetch:
+            c.wait()
+        acts_in[...] = acts_product(weight_in[...], og_in[...])
+        back = pltpu.make_async_copy(acts_in, acts_out, acts_sem.at[2])
+        back.start()
+        back.wait()
+
     for c in copies:
         c.wait()
 
 
-def merge_call(got, first, first_steps, rows, cols):
+def merge_call(got, first, first_steps, weight, og, acts_early):
+    rows, cols = weight.shape
+    toks = og.shape[0]
     vm = pl.BlockSpec(memory_space=pltpu.VMEM)
     anyw = pl.BlockSpec(memory_space=pl.ANY)
     islands = got.shape[0]
     return pl.pallas_call(
         merge_kernel,
-        in_specs=[vm] * 5,
-        out_specs=anyw,
-        out_shape=jax.ShapeDtypeStruct((rows, cols), BF),
+        in_specs=[vm] * 5 + [anyw] * 3,
+        out_specs=[anyw, anyw],
+        out_shape=[
+            jax.ShapeDtypeStruct((rows, cols), BF),
+            jax.ShapeDtypeStruct((rows, toks), BF),
+        ],
+        input_output_aliases={7: 1},
         scratch_shapes=[
             pltpu.VMEM((1, rows * cols), F32),
             pltpu.VMEM((islands // SHARE, 128), jnp.int32),
             pltpu.SMEM((islands // SHARE, 128), jnp.int32),
             pltpu.VMEM((rows, cols), BF),
+            pltpu.VMEM((rows, cols), BF),
+            pltpu.VMEM((toks, cols), BF),
+            pltpu.VMEM((rows, toks), BF),
             pltpu.SemaphoreType.DMA,
             pltpu.SemaphoreType.DMA((cols // (256 * GROUP),)),
+            pltpu.SemaphoreType.DMA((3,)),
         ],
         compiler_params=pltpu.CompilerParams(vmem_limit_bytes=32 * MIB),
         cost_estimate=pl.CostEstimate(flops=1_000_000_000, bytes_accessed=2 * MIB, transcendentals=0),
         name="merge_update",
-    )(got, first, first_steps, INV_LEFT3_MIRROR, INV_RIGHT2)
+    )(
+        got, first, first_steps, INV_LEFT3_MIRROR, INV_RIGHT2,
+        *[pltpu.with_memory_space_constraint(x, pltpu.HBM) for x in (weight, og, acts_early)]
+    )
 
 
 def on_device(weight, acts_t, out_grad, momentum, chosen, counts, steps):
@@ -389,7 +433,7 @@
     swapped = lax.ppermute(got, "island", other_core)
 
     first, first_steps, momentum_next = scatter_call(got, factor, rest_m, rest_g)
-    update = merge_call(swapped, first, first_steps, rows, cols)
+    update, acts_grad = merge_call(swapped, first, first_steps, weight, out_grad, acts_grad)
     return (update, momentum_next[None], acts_grad)
 
 

time: 44.4 us -> 42.9 us (0.966)
  blocking collectives: 21.5 us -> 20.3 us
    all_to_all x1, blocking collectives: 21.5 us -> 20.3 us  [on_device(): lax.all_to_all(sent, 'island', 0, 0, tiled=True, axis_index_groups=same_c...]
where the time goes in v5:
time: 42.9 us; the launch traced here: 42.8 us
  blocking collectives  20.3 us (47%)
  Pallas kernels  12 us (28%)
  starting transfers between devices  7.98 us (19%)
  between operations  2.12 us (5%)
    all_to_all x1, blocking collectives, on_device(): lax.all_to_all(sent, 'island', 0, 0, tiled=True, axis_index_groups=same_c...  20.3 us
    ppermute x1, starting transfers between devices, on_device(): swapped = lax.ppermute(got, 'island', other_core)  3.95 us
    pallas_call x1, Pallas kernels, merge_call(): pl.pallas_call(merge_kernel, in_specs=[vm] * 5 + [anyw] * 3, out_specs=[a...  3.66 us
    pallas_call x1, Pallas kernels, grad_call(): pl.pallas_call(grad_kernel, in_specs=[anyw] * 3, out_specs=[vm] * 4, out_...  2.89 us
    ppermute x1, starting transfers between devices, on_device(): lax.ppermute(squares, 'shard', [(i, i ^ 1) for i in range(shards)])  2.13 us
    pallas_call x1, Pallas kernels, coef_call(): pl.pallas_call(coef_kernel, in_specs=[sm, sm] + [vm] * 7, out_specs=[vm]...  2 us
    pallas_call x1, Pallas kernels, acts_grad_call(): pl.pallas_call(acts_grad_kernel, in_specs=[vm, vm], out_specs=vm, out_sha...  1.91 us
    ppermute x1, starting transfers between devices, on_device(): lax.ppermute(squares, 'shard', [(i, i ^ 3) for i in range(shards)])  1.9 us
  transfers between devices with their start and end apart: 3, of which 0 were waited for; matrix products, arithmetic and copies ran while one was open for 0% of the time, Pallas kernels for 13%

profile of v5, /device:TPU:1, one launch (start us, length us, event | category | flops | bytes accessed | tf_op | source)
XLA Modules:
  0.0 42.8 jit_solution(1726244479112845691)
XLA Ops:
  0.6 0.0 copy-start.8
  0.6 2.9 %weight_grad.1 = (f32[64,8192]{1,0:T(8,128)S(1)}, f32[1,128]{1,0:T(1,128)S(1)}, bf16[256,8192]{1,0:T(8,128)(2,1)S(1)}, bf16[64,8192]{1,0:T(8,128)(2,1)S(1)}) custom-call(bf16[64,256]{1,0:T(8,128)(2,1)} %acts.1, bf16[256,8192]{1,0:T(8,128)(2,1)} %og.3, bf16[64,8192]{1,0:T(8,128)(2,1)} %weight.3), custom_call_target="tpu_custom_call" | custom-call | flops 268435456 | bytes 6291456 | tf_op jit(solution)/shard_map/weight_grad/pallas_call | solution.py:99
  3.5 2.1 %collective-permute-start = (f32[1,128]{1,0:T(1,128)S(1)}, f32[1,128]{1,0:T(1,128)S(1)}, u32[]{:S(2)}, u32[]{:S(2)}) collective-permute-start(f32[1,128]{1,0:T(1,128)S(1)} %get-tuple-element.24), channel_id=1, source_target_pairs={{0,1},{1,0},{2,3},{3,2},{4,5},{5,4},{6,7},{7,6},{8,9},{9,8},{10,11... | collective-permute-start | bytes 1544 | tf_op jit(solution)/shard_map/ppermute | solution.py:416
  6.3 0.0 copy-done.8
  6.4 0.1 pad_maximum_fusion
  6.4 0.0 copy-start
  6.4 0.0 copy-start.2
  6.4 0.0 copy-start.3
  6.4 0.0 copy-start.5
  6.4 0.0 copy-start.6
  6.5 0.0 copy-start.7
  6.5 1.9 %acts_grad.1.acts_early = bf16[64,256]{1,0:T(8,128)(2,1)} custom-call(bf16[64,8192]{1,0:T(8,128)(2,1)S(1)} %get-tuple-element.25.weight, bf16[256,8192]{1,0:T(8,128)(2,1)S(1)} %get-tuple-element.26.og), custom_call_target="tpu_custom_call" | custom-call | flops 268435456 | bytes 5242880 | tf_op jit(solution)/shard_map/acts_grad/pallas_call | solution.py:138
  9.0 0.0 collective-permute-done
  9.1 1.9 %collective-permute-start.1 = (f32[1,128]{1,0:T(1,128)S(1)}, f32[1,128]{1,0:T(1,128)S(1)}, u32[]{:S(2)}, u32[]{:S(2)}) collective-permute-start(f32[1,128]{1,0:T(1,128)S(1)} %add.21), channel_id=1, source_target_pairs={{0,3},{1,2},{2,1},{3,0},{4,7},{5,6},{6,5},{7,4},{8,11},{9,10},{10,... | collective-permute-start | bytes 1544 | tf_op jit(solution)/shard_map/ppermute | solution.py:419
  11.0 0.0 copy-done
  11.0 0.0 copy-done.2
  11.0 0.0 copy-done.3
  11.0 0.0 copy-done.5
  11.0 0.0 copy-done.6
  11.0 0.0 copy-done.7
  11.0 2.0 %selected_coefs.1 = (f32[16,128]{1,0:T(8,128)S(1)}, f32[16,128]{1,0:T(8,128)S(1)}, f32[64,8192]{1,0:T(8,128)S(1)}, f32[64,8192]{1,0:T(8,128)S(1)}) custom-call(s32[16]{0:T(128)S(1)} %get-tuple-element.46.picks, s32[1]{0:T(128)} %bitcast.11.counts, bf16[64,8192]{1,0:T(8,128)(2,1)S(1)} %bitcast.12, f32[64,8192]{1,0:T(8,128)S(1)} %get-tuple-element.28.grad, ...), custom_call_target="tpu_custom_call" | custom-call | flops 300000000 | bytes 8388608 | tf_op jit(solution)/shard_map/selected_coefs/pallas_call | solution.py:205
  13.0 0.0 collective-permute-done.1
  13.1 0.1 broadcast_in_dim.21
  13.2 20.3 %all_to_all.5.got = f32[32,1,2176]{2,1,0:T(1,128)S(1)} all-to-all(f32[32,1,2176]{2,1,0:T(1,128)S(1)} %broadcast_in_dim.21), channel_id=1, replica_groups={{0,8,16,24,32,40,48,56,64,72,80,88,96,104,112,120,128,136,144,152,160,1..., dimensions={0} | all-to-all | bytes 557056 | tf_op jit(solution)/shard_map/all_to_all | solution.py:432
  33.5 3.9 %collective-permute-start.2 = (f32[32,1,2176]{2,1,0:T(1,128)S(1)}, f32[32,1,2176]{2,1,0:T(1,128)S(1)}, u32[]{:S(2)}, u32[]{:S(2)}) collective-permute-start(f32[32,1,2176]{2,1,0:T(1,128)S(1)} %all_to_all.5.got), channel_id=1, source_target_pairs={{0,4},{4,0},{8,12},{12,8},{16,20},{20,16},{24,28},{28,24},{32,36},... | collective-permute-start | bytes 835592 | tf_op jit(solution)/shard_map/ppermute | solution.py:433
  37.5 0.0 copy-start.1
  37.5 0.0 copy-start.4
  37.5 1.6 %scatter_own.1 = (f32[1,524288]{1,0:T(1,128)S(1)}, f32[1,128]{1,0:T(1,128)S(1)}, bf16[64,8192]{1,0:T(8,128)(2,1)}) custom-call(f32[32,1,2176]{2,1,0:T(1,128)S(1)} %all_to_all.5.got, f32[1,128]{1,0:T(1,128)S(1)} %rsqrt_minimum_fusion.factor, f32[64,8192]{1,0:T(8,128)S(1)} %get-tuple-element.37.rest_m, f32[64,8192]{1,0:T(8,128)S(1)} %get-tuple-element.38.rest_g), custom_call_target="tpu_custom_call" | custom-call | flops 300000000 | bytes 8388608 | tf_op jit(solution)/shard_map/scatter_own/pallas_call | solution.py:289
  39.1 0.0 collective-permute-done.2.got
  39.1 0.0 copy-done.1
  39.1 0.0 copy-done.4
  39.1 3.7 %merge_update.1 = (bf16[64,8192]{1,0:T(8,128)(2,1)}, bf16[64,256]{1,0:T(8,128)(2,1)}) custom-call(f32[32,1,2176]{2,1,0:T(1,128)S(1)} %collective-permute-done.2.got, f32[1,524288]{1,0:T(1,128)S(1)} %get-tuple-element.39.first, f32[1,128]{1,0:T(1,128)S(1)} %get-tuple-element.40.first_steps, ...), custom_call_target="tpu_custom_call", output_to_operand_aliasing={{1}: (7, {})} | custom-call | flops 1000000000 | bytes 2097152 | tf_op jit(solution)/shard_map/merge_update/pallas_call | solution.py:373
  (8 shorter events, 0.1 us)
Async XLA Ops:
  0.6 5.7 %copy-start.8 = (s32[1,16]{1,0:T(1,128)S(1)}, s32[1,16]{1,0:T(1,128)}, u32[]{:S(2)}) copy-start(s32[1,16]{1,0:T(1,128)} %param.18) | copy-start | bytes 196
  3.5 5.5 %collective-permute-start = (f32[1,128]{1,0:T(1,128)S(1)}, f32[1,128]{1,0:T(1,128)S(1)}, u32[]{:S(2)}, u32[]{:S(2)}) collective-permute-start(f32[1,128]{1,0:T(1,128)S(1)} %get-tuple-element.24), channel_id=1, source_target_pairs={{0,1},{1,0},{2,3},{3,2},{4,5},{5,4},{6,7},{7,6},{8,9},{9,8},{10,11... | collective-permute-start | bytes 1544 | tf_op jit(solution)/shard_map/ppermute | solution.py:416
  6.4 4.5 %copy-start = (bf16[1,64,8192]{2,1,0:T(8,128)(2,1)S(1)}, bf16[1,64,8192]{2,1,0:T(8,128)(2,1)}, u32[]{:S(2)}) copy-start(bf16[1,64,8192]{2,1,0:T(8,128)(2,1)} %param.17) | copy-start | bytes 3145732
  6.4 4.5 %copy-start.2 = (bf16[384,128]{1,0:T(8,128)(2,1)S(1)}, bf16[384,128]{1,0:T(8,128)(2,1)}, u32[]{:S(2)}) copy-start(bf16[384,128]{1,0:T(8,128)(2,1)} %constant.44.clone.back_right3) | copy-start | bytes 294916
  6.4 4.5 %copy-start.3 = (bf16[384,128]{1,0:T(8,128)(2,1)S(1)}, bf16[384,128]{1,0:T(8,128)(2,1)}, u32[]{:S(2)}) copy-start(bf16[384,128]{1,0:T(8,128)(2,1)} %constant.42.clone.right3) | copy-start | bytes 294916
  6.4 4.5 %copy-start.5 = (bf16[64,192]{1,0:T(8,128)(2,1)S(1)}, bf16[64,192]{1,0:T(8,128)(2,1)}, u32[]{:S(2)}) copy-start(bf16[64,192]{1,0:T(8,128)(2,1)} %constant.43.clone.back_left3) | copy-start | bytes 73732
  6.4 4.5 %copy-start.6 = (bf16[64,192]{1,0:T(8,128)(2,1)S(1)}, bf16[64,192]{1,0:T(8,128)(2,1)}, u32[]{:S(2)}) copy-start(bf16[64,192]{1,0:T(8,128)(2,1)} %constant.41.clone.left3) | copy-start | bytes 73732
  6.5 4.5 %copy-start.7 = (bf16[64,128]{1,0:T(8,128)(2,1)S(1)}, bf16[64,128]{1,0:T(8,128)(2,1)}, u32[]{:S(2)}) copy-start(bf16[64,128]{1,0:T(8,128)(2,1)} %constant.40.clone.left2) | copy-start | bytes 49156
  9.1 3.9 %collective-permute-start.1 = (f32[1,128]{1,0:T(1,128)S(1)}, f32[1,128]{1,0:T(1,128)S(1)}, u32[]{:S(2)}, u32[]{:S(2)}) collective-permute-start(f32[1,128]{1,0:T(1,128)S(1)} %add.21), channel_id=1, source_target_pairs={{0,3},{1,2},{2,1},{3,0},{4,7},{5,6},{6,5},{7,4},{8,11},{9,10},{10,... | collective-permute-start | bytes 1544 | tf_op jit(solution)/shard_map/ppermute | solution.py:419
  33.5 5.6 %collective-permute-start.2 = (f32[32,1,2176]{2,1,0:T(1,128)S(1)}, f32[32,1,2176]{2,1,0:T(1,128)S(1)}, u32[]{:S(2)}, u32[]{:S(2)}) collective-permute-start(f32[32,1,2176]{2,1,0:T(1,128)S(1)} %all_to_all.5.got), channel_id=1, source_target_pairs={{0,4},{4,0},{8,12},{12,8},{16,20},{20,16},{24,28},{28,24},{32,36},... | collective-permute-start | bytes 835592 | tf_op jit(solution)/shard_map/ppermute | solution.py:433
  37.5 1.6 %copy-start.1 = (bf16[256,256]{1,0:T(8,128)(2,1)S(1)}, bf16[256,256]{1,0:T(8,128)(2,1)}, u32[]{:S(2)}) copy-start(bf16[256,256]{1,0:T(8,128)(2,1)} %constant.46.clone.right2) | copy-start | bytes 393220
  37.5 1.6 %copy-start.4 = (bf16[64,192]{1,0:T(8,128)(2,1)S(1)}, bf16[64,192]{1,0:T(8,128)(2,1)}, u32[]{:S(2)}) copy-start(bf16[64,192]{1,0:T(8,128)(2,1)} %constant.45.clone.left3) | copy-start | bytes 73732

commit v6 on v5

--- a/solution.py
+++ b/solution.py
@@ -405,7 +405,7 @@
     islands = lax.axis_size("island")
     shards = lax.axis_size("shard")
     half = islands // 2
-    same_core = [[2 * i + c for i in range(half)] for c in range(2)]
+    same_core = [[2 * i + c for i in reversed(range(half))] for c in range(2)]
     other_core = [(i, i ^ 1) for i in range(islands)]
     momentum = momentum[0]
 

time: 42.9 us -> 40.4 us (0.942)
  blocking collectives: 20.3 us -> 17.9 us
    all_to_all x1, blocking collectives: 20.3 us -> 17.9 us  [on_device(): lax.all_to_all(sent, 'island', 0, 0, tiled=True, axis_index_groups=same_c...]
  transfers between devices with their start and end apart: 3 -> 3, of which waited for: 0 -> 0; matrix products, arithmetic and copies ran while one was open for 0% -> 0% of each run, Pallas kernels for 13% -> 14%
where the time goes in v6:
time: 40.4 us; the launch traced here: 40.3 us
  blocking collectives  17.9 us (44%)
  Pallas kernels  12 us (30%)
  starting transfers between devices  7.89 us (20%)
  between operations  2.12 us (5%)
    all_to_all x1, blocking collectives, on_device(): lax.all_to_all(sent, 'island', 0, 0, tiled=True, axis_index_groups=same_c...  17.9 us
    ppermute x1, starting transfers between devices, on_device(): swapped = lax.ppermute(got, 'island', other_core)  3.86 us
    pallas_call x1, Pallas kernels, merge_call(): pl.pallas_call(merge_kernel, in_specs=[vm] * 5 + [anyw] * 3, out_specs=[a...  3.67 us
    pallas_call x1, Pallas kernels, grad_call(): pl.pallas_call(grad_kernel, in_specs=[anyw] * 3, out_specs=[vm] * 4, out_...  2.89 us
    ppermute x1, starting transfers between devices, on_device(): lax.ppermute(squares, 'shard', [(i, i ^ 1) for i in range(shards)])  2.13 us
    pallas_call x1, Pallas kernels, coef_call(): pl.pallas_call(coef_kernel, in_specs=[sm, sm] + [vm] * 7, out_specs=[vm]...  1.99 us
    pallas_call x1, Pallas kernels, acts_grad_call(): pl.pallas_call(acts_grad_kernel, in_specs=[vm, vm], out_specs=vm, out_sha...  1.91 us
    ppermute x1, starting transfers between devices, on_device(): lax.ppermute(squares, 'shard', [(i, i ^ 3) for i in range(shards)])  1.9 us
  transfers between devices with their start and end apart: 3, of which 0 were waited for; matrix products, arithmetic and copies ran while one was open for 0% of the time, Pallas kernels for 14%

profile of v6, /device:TPU:1, one launch (start us, length us, event | category | flops | bytes accessed | tf_op | source)
XLA Modules:
  0.0 40.3 jit_solution(17712910815283808490)
XLA Ops:
  0.6 0.0 copy-start.8
  0.6 2.9 %weight_grad.1 = (f32[64,8192]{1,0:T(8,128)S(1)}, f32[1,128]{1,0:T(1,128)S(1)}, bf16[256,8192]{1,0:T(8,128)(2,1)S(1)}, bf16[64,8192]{1,0:T(8,128)(2,1)S(1)}) custom-call(bf16[64,256]{1,0:T(8,128)(2,1)} %acts.1, bf16[256,8192]{1,0:T(8,128)(2,1)} %og.3, bf16[64,8192]{1,0:T(8,128)(2,1)} %weight.3), custom_call_target="tpu_custom_call" | custom-call | flops 268435456 | bytes 6291456 | tf_op jit(solution)/shard_map/weight_grad/pallas_call | solution.py:99
  3.5 2.1 %collective-permute-start = (f32[1,128]{1,0:T(1,128)S(1)}, f32[1,128]{1,0:T(1,128)S(1)}, u32[]{:S(2)}, u32[]{:S(2)}) collective-permute-start(f32[1,128]{1,0:T(1,128)S(1)} %get-tuple-element.24), channel_id=1, source_target_pairs={{0,1},{1,0},{2,3},{3,2},{4,5},{5,4},{6,7},{7,6},{8,9},{9,8},{10,11... | collective-permute-start | bytes 1544 | tf_op jit(solution)/shard_map/ppermute | solution.py:416
  6.3 0.0 copy-done.8
  6.4 0.1 pad_maximum_fusion
  6.4 0.0 copy-start
  6.4 0.0 copy-start.2
  6.4 0.0 copy-start.3
  6.4 0.0 copy-start.5
  6.4 0.0 copy-start.6
  6.5 0.0 copy-start.7
  6.5 1.9 %acts_grad.1.acts_early = bf16[64,256]{1,0:T(8,128)(2,1)} custom-call(bf16[64,8192]{1,0:T(8,128)(2,1)S(1)} %get-tuple-element.25.weight, bf16[256,8192]{1,0:T(8,128)(2,1)S(1)} %get-tuple-element.26.og), custom_call_target="tpu_custom_call" | custom-call | flops 268435456 | bytes 5242880 | tf_op jit(solution)/shard_map/acts_grad/pallas_call | solution.py:138
  9.0 0.0 collective-permute-done
  9.1 1.9 %collective-permute-start.1 = (f32[1,128]{1,0:T(1,128)S(1)}, f32[1,128]{1,0:T(1,128)S(1)}, u32[]{:S(2)}, u32[]{:S(2)}) collective-permute-start(f32[1,128]{1,0:T(1,128)S(1)} %add.21), channel_id=1, source_target_pairs={{0,3},{1,2},{2,1},{3,0},{4,7},{5,6},{6,5},{7,4},{8,11},{9,10},{10,... | collective-permute-start | bytes 1544 | tf_op jit(solution)/shard_map/ppermute | solution.py:419
  11.0 0.0 copy-done
  11.0 0.0 copy-done.2
  11.0 0.0 copy-done.3
  11.0 0.0 copy-done.5
  11.0 0.0 copy-done.6
  11.0 0.0 copy-done.7
  11.0 2.0 %selected_coefs.1 = (f32[16,128]{1,0:T(8,128)S(1)}, f32[16,128]{1,0:T(8,128)S(1)}, f32[64,8192]{1,0:T(8,128)S(1)}, f32[64,8192]{1,0:T(8,128)S(1)}) custom-call(s32[16]{0:T(128)S(1)} %get-tuple-element.46.picks, s32[1]{0:T(128)} %bitcast.11.counts, bf16[64,8192]{1,0:T(8,128)(2,1)S(1)} %bitcast.12, f32[64,8192]{1,0:T(8,128)S(1)} %get-tuple-element.28.grad, ...), custom_call_target="tpu_custom_call" | custom-call | flops 300000000 | bytes 8388608 | tf_op jit(solution)/shard_map/selected_coefs/pallas_call | solution.py:205
  13.0 0.0 collective-permute-done.1
  13.1 0.1 broadcast_in_dim.21
  13.2 17.9 %all_to_all.5.got = f32[32,1,2176]{2,1,0:T(1,128)S(1)} all-to-all(f32[32,1,2176]{2,1,0:T(1,128)S(1)} %broadcast_in_dim.21), channel_id=1, replica_groups={{248,240,232,224,216,208,200,192,184,176,168,160,152,144,136,128,120,11..., dimensions={0} | all-to-all | bytes 557056 | tf_op jit(solution)/shard_map/all_to_all | solution.py:432
  31.1 3.9 %collective-permute-start.2 = (f32[32,1,2176]{2,1,0:T(1,128)S(1)}, f32[32,1,2176]{2,1,0:T(1,128)S(1)}, u32[]{:S(2)}, u32[]{:S(2)}) collective-permute-start(f32[32,1,2176]{2,1,0:T(1,128)S(1)} %all_to_all.5.got), channel_id=1, source_target_pairs={{0,4},{4,0},{8,12},{12,8},{16,20},{20,16},{24,28},{28,24},{32,36},... | collective-permute-start | bytes 835592 | tf_op jit(solution)/shard_map/ppermute | solution.py:433
  35.0 0.0 copy-start.1
  35.0 0.0 copy-start.4
  35.0 1.6 %scatter_own.1 = (f32[1,524288]{1,0:T(1,128)S(1)}, f32[1,128]{1,0:T(1,128)S(1)}, bf16[64,8192]{1,0:T(8,128)(2,1)}) custom-call(f32[32,1,2176]{2,1,0:T(1,128)S(1)} %all_to_all.5.got, f32[1,128]{1,0:T(1,128)S(1)} %rsqrt_minimum_fusion.factor, f32[64,8192]{1,0:T(8,128)S(1)} %get-tuple-element.37.rest_m, f32[64,8192]{1,0:T(8,128)S(1)} %get-tuple-element.38.rest_g), custom_call_target="tpu_custom_call" | custom-call | flops 300000000 | bytes 8388608 | tf_op jit(solution)/shard_map/scatter_own/pallas_call | solution.py:289
  36.6 0.0 collective-permute-done.2.got
  36.6 0.0 copy-done.1
  36.6 0.0 copy-done.4
  36.6 3.7 %merge_update.1 = (bf16[64,8192]{1,0:T(8,128)(2,1)}, bf16[64,256]{1,0:T(8,128)(2,1)}) custom-call(f32[32,1,2176]{2,1,0:T(1,128)S(1)} %collective-permute-done.2.got, f32[1,524288]{1,0:T(1,128)S(1)} %get-tuple-element.39.first, f32[1,128]{1,0:T(1,128)S(1)} %get-tuple-element.40.first_steps, ...), custom_call_target="tpu_custom_call", output_to_operand_aliasing={{1}: (7, {})} | custom-call | flops 1000000000 | bytes 2097152 | tf_op jit(solution)/shard_map/merge_update/pallas_call | solution.py:373
  (8 shorter events, 0.1 us)
Async XLA Ops:
  0.6 5.7 %copy-start.8 = (s32[1,16]{1,0:T(1,128)S(1)}, s32[1,16]{1,0:T(1,128)}, u32[]{:S(2)}) copy-start(s32[1,16]{1,0:T(1,128)} %param.18) | copy-start | bytes 196
  3.5 5.5 %collective-permute-start = (f32[1,128]{1,0:T(1,128)S(1)}, f32[1,128]{1,0:T(1,128)S(1)}, u32[]{:S(2)}, u32[]{:S(2)}) collective-permute-start(f32[1,128]{1,0:T(1,128)S(1)} %get-tuple-element.24), channel_id=1, source_target_pairs={{0,1},{1,0},{2,3},{3,2},{4,5},{5,4},{6,7},{7,6},{8,9},{9,8},{10,11... | collective-permute-start | bytes 1544 | tf_op jit(solution)/shard_map/ppermute | solution.py:416
  6.4 4.5 %copy-start = (bf16[1,64,8192]{2,1,0:T(8,128)(2,1)S(1)}, bf16[1,64,8192]{2,1,0:T(8,128)(2,1)}, u32[]{:S(2)}) copy-start(bf16[1,64,8192]{2,1,0:T(8,128)(2,1)} %param.17) | copy-start | bytes 3145732
  6.4 4.5 %copy-start.2 = (bf16[384,128]{1,0:T(8,128)(2,1)S(1)}, bf16[384,128]{1,0:T(8,128)(2,1)}, u32[]{:S(2)}) copy-start(bf16[384,128]{1,0:T(8,128)(2,1)} %constant.44.clone.back_right3) | copy-start | bytes 294916
  6.4 4.5 %copy-start.3 = (bf16[384,128]{1,0:T(8,128)(2,1)S(1)}, bf16[384,128]{1,0:T(8,128)(2,1)}, u32[]{:S(2)}) copy-start(bf16[384,128]{1,0:T(8,128)(2,1)} %constant.42.clone.right3) | copy-start | bytes 294916
  6.4 4.5 %copy-start.5 = (bf16[64,192]{1,0:T(8,128)(2,1)S(1)}, bf16[64,192]{1,0:T(8,128)(2,1)}, u32[]{:S(2)}) copy-start(bf16[64,192]{1,0:T(8,128)(2,1)} %constant.43.clone.back_left3) | copy-start | bytes 73732
  6.4 4.5 %copy-start.6 = (bf16[64,192]{1,0:T(8,128)(2,1)S(1)}, bf16[64,192]{1,0:T(8,128)(2,1)}, u32[]{:S(2)}) copy-start(bf16[64,192]{1,0:T(8,128)(2,1)} %constant.41.clone.left3) | copy-start | bytes 73732
  6.5 4.5 %copy-start.7 = (bf16[64,128]{1,0:T(8,128)(2,1)S(1)}, bf16[64,128]{1,0:T(8,128)(2,1)}, u32[]{:S(2)}) copy-start(bf16[64,128]{1,0:T(8,128)(2,1)} %constant.40.clone.left2) | copy-start | bytes 49156
  9.1 3.9 %collective-permute-start.1 = (f32[1,128]{1,0:T(1,128)S(1)}, f32[1,128]{1,0:T(1,128)S(1)}, u32[]{:S(2)}, u32[]{:S(2)}) collective-permute-start(f32[1,128]{1,0:T(1,128)S(1)} %add.21), channel_id=1, source_target_pairs={{0,3},{1,2},{2,1},{3,0},{4,7},{5,6},{6,5},{7,4},{8,11},{9,10},{10,... | collective-permute-start | bytes 1544 | tf_op jit(solution)/shard_map/ppermute | solution.py:419
  31.1 5.5 %collective-permute-start.2 = (f32[32,1,2176]{2,1,0:T(1,128)S(1)}, f32[32,1,2176]{2,1,0:T(1,128)S(1)}, u32[]{:S(2)}, u32[]{:S(2)}) collective-permute-start(f32[32,1,2176]{2,1,0:T(1,128)S(1)} %all_to_all.5.got), channel_id=1, source_target_pairs={{0,4},{4,0},{8,12},{12,8},{16,20},{20,16},{24,28},{28,24},{32,36},... | collective-permute-start | bytes 835592 | tf_op jit(solution)/shard_map/ppermute | solution.py:433
  35.0 1.6 %copy-start.1 = (bf16[256,256]{1,0:T(8,128)(2,1)S(1)}, bf16[256,256]{1,0:T(8,128)(2,1)}, u32[]{:S(2)}) copy-start(bf16[256,256]{1,0:T(8,128)(2,1)} %constant.46.clone.right2) | copy-start | bytes 393220
  35.0 1.6 %copy-start.4 = (bf16[64,192]{1,0:T(8,128)(2,1)S(1)}, bf16[64,192]{1,0:T(8,128)(2,1)}, u32[]{:S(2)}) copy-start(bf16[64,192]{1,0:T(8,128)(2,1)} %constant.45.clone.left3) | copy-start | bytes 73732

commit v7 on v6

--- a/solution.py
+++ b/solution.py
@@ -405,7 +405,7 @@
     islands = lax.axis_size("island")
     shards = lax.axis_size("shard")
     half = islands // 2
-    same_core = [[2 * i + c for i in reversed(range(half))] for c in range(2)]
+    same_core = [[2 * (4 * z + y) + c for z in (4, 5, 6, 7, 0, 1, 2, 3) for y in (3, 2, 1, 0)] for c in range(2)]
     other_core = [(i, i ^ 1) for i in range(islands)]
     momentum = momentum[0]
 

time: 40.4 us -> 38.6 us (0.955)
  blocking collectives: 17.9 us -> 16.6 us
  starting transfers between devices: 7.89 us -> 7.32 us
    all_to_all x1, blocking collectives: 17.9 us -> 16.6 us  [on_device(): lax.all_to_all(sent, 'island', 0, 0, tiled=True, axis_index_groups=same_c...]
    ppermute x1, starting transfers between devices: 3.86 us -> 3.3 us  [on_device(): swapped = lax.ppermute(got, 'island', other_core)]
where the time goes in v7:
time: 38.6 us; the launch traced here: 38.5 us
  blocking collectives  16.6 us (43%)
  Pallas kernels  12.1 us (31%)
  starting transfers between devices  7.32 us (19%)
  between operations  2.12 us (5%)
    all_to_all x1, blocking collectives, on_device(): lax.all_to_all(sent, 'island', 0, 0, tiled=True, axis_index_groups=same_c...  16.6 us
    pallas_call x1, Pallas kernels, merge_call(): pl.pallas_call(merge_kernel, in_specs=[vm] * 5 + [anyw] * 3, out_specs=[a...  3.66 us
    ppermute x1, starting transfers between devices, on_device(): swapped = lax.ppermute(got, 'island', other_core)  3.3 us
    pallas_call x1, Pallas kernels, grad_call(): pl.pallas_call(grad_kernel, in_specs=[anyw] * 3, out_specs=[vm] * 4, out_...  2.89 us
    ppermute x1, starting transfers between devices, on_device(): lax.ppermute(squares, 'shard', [(i, i ^ 1) for i in range(shards)])  2.13 us
    pallas_call x1, Pallas kernels, coef_call(): pl.pallas_call(coef_kernel, in_specs=[sm, sm] + [vm] * 7, out_specs=[vm]...  2.01 us
    pallas_call x1, Pallas kernels, acts_grad_call(): pl.pallas_call(acts_grad_kernel, in_specs=[vm, vm], out_specs=vm, out_sha...  1.91 us
    ppermute x1, starting transfers between devices, on_device(): lax.ppermute(squares, 'shard', [(i, i ^ 3) for i in range(shards)])  1.9 us
  transfers between devices with their start and end apart: 3, of which 0 were waited for; matrix products, arithmetic and copies ran while one was open for 0% of the time, Pallas kernels for 14%

profile of v7, /device:TPU:1, one launch (start us, length us, event | category | flops | bytes accessed | tf_op | source)
XLA Modules:
  0.0 38.5 jit_solution(9758404542269429320)
XLA Ops:
  0.6 0.0 copy-start.8
  0.6 2.9 %weight_grad.1 = (f32[64,8192]{1,0:T(8,128)S(1)}, f32[1,128]{1,0:T(1,128)S(1)}, bf16[256,8192]{1,0:T(8,128)(2,1)S(1)}, bf16[64,8192]{1,0:T(8,128)(2,1)S(1)}) custom-call(bf16[64,256]{1,0:T(8,128)(2,1)} %acts.1, bf16[256,8192]{1,0:T(8,128)(2,1)} %og.3, bf16[64,8192]{1,0:T(8,128)(2,1)} %weight.3), custom_call_target="tpu_custom_call" | custom-call | flops 268435456 | bytes 6291456 | tf_op jit(solution)/shard_map/weight_grad/pallas_call | solution.py:99
  3.5 2.1 %collective-permute-start = (f32[1,128]{1,0:T(1,128)S(1)}, f32[1,128]{1,0:T(1,128)S(1)}, u32[]{:S(2)}, u32[]{:S(2)}) collective-permute-start(f32[1,128]{1,0:T(1,128)S(1)} %get-tuple-element.24), channel_id=1, source_target_pairs={{0,1},{1,0},{2,3},{3,2},{4,5},{5,4},{6,7},{7,6},{8,9},{9,8},{10,11... | collective-permute-start | bytes 1544 | tf_op jit(solution)/shard_map/ppermute | solution.py:416
  6.3 0.0 copy-done.8
  6.4 0.1 pad_maximum_fusion
  6.4 0.0 copy-start
  6.4 0.0 copy-start.2
  6.4 0.0 copy-start.3
  6.4 0.0 copy-start.5
  6.4 0.0 copy-start.6
  6.5 0.0 copy-start.7
  6.5 1.9 %acts_grad.1.acts_early = bf16[64,256]{1,0:T(8,128)(2,1)} custom-call(bf16[64,8192]{1,0:T(8,128)(2,1)S(1)} %get-tuple-element.25.weight, bf16[256,8192]{1,0:T(8,128)(2,1)S(1)} %get-tuple-element.26.og), custom_call_target="tpu_custom_call" | custom-call | flops 268435456 | bytes 5242880 | tf_op jit(solution)/shard_map/acts_grad/pallas_call | solution.py:138
  9.0 0.0 collective-permute-done
  9.1 1.9 %collective-permute-start.1 = (f32[1,128]{1,0:T(1,128)S(1)}, f32[1,128]{1,0:T(1,128)S(1)}, u32[]{:S(2)}, u32[]{:S(2)}) collective-permute-start(f32[1,128]{1,0:T(1,128)S(1)} %add.21), channel_id=1, source_target_pairs={{0,3},{1,2},{2,1},{3,0},{4,7},{5,6},{6,5},{7,4},{8,11},{9,10},{10,... | collective-permute-start | bytes 1544 | tf_op jit(solution)/shard_map/ppermute | solution.py:419
  11.0 0.0 copy-done
  11.0 0.0 copy-done.2
  11.0 0.0 copy-done.3
  11.0 0.0 copy-done.5
  11.0 0.0 copy-done.6
  11.0 0.0 copy-done.7
  11.0 2.0 %selected_coefs.1 = (f32[16,128]{1,0:T(8,128)S(1)}, f32[16,128]{1,0:T(8,128)S(1)}, f32[64,8192]{1,0:T(8,128)S(1)}, f32[64,8192]{1,0:T(8,128)S(1)}) custom-call(s32[16]{0:T(128)S(1)} %get-tuple-element.46.picks, s32[1]{0:T(128)} %bitcast.11.counts, bf16[64,8192]{1,0:T(8,128)(2,1)S(1)} %bitcast.12, f32[64,8192]{1,0:T(8,128)S(1)} %get-tuple-element.28.grad, ...), custom_call_target="tpu_custom_call" | custom-call | flops 300000000 | bytes 8388608 | tf_op jit(solution)/shard_map/selected_coefs/pallas_call | solution.py:205
  13.0 0.0 collective-permute-done.1
  13.1 0.1 broadcast_in_dim.21
  13.3 16.6 %all_to_all.5.got = f32[32,1,2176]{2,1,0:T(1,128)S(1)} all-to-all(f32[32,1,2176]{2,1,0:T(1,128)S(1)} %broadcast_in_dim.21), channel_id=1, replica_groups={{152,144,136,128,184,176,168,160,216,208,200,192,248,240,232,224,24,16,..., dimensions={0} | all-to-all | bytes 557056 | tf_op jit(solution)/shard_map/all_to_all | solution.py:432
  29.9 3.3 %collective-permute-start.2 = (f32[32,1,2176]{2,1,0:T(1,128)S(1)}, f32[32,1,2176]{2,1,0:T(1,128)S(1)}, u32[]{:S(2)}, u32[]{:S(2)}) collective-permute-start(f32[32,1,2176]{2,1,0:T(1,128)S(1)} %all_to_all.5.got), channel_id=1, source_target_pairs={{0,4},{4,0},{8,12},{12,8},{16,20},{20,16},{24,28},{28,24},{32,36},... | collective-permute-start | bytes 835592 | tf_op jit(solution)/shard_map/ppermute | solution.py:433
  33.2 0.0 copy-start.1
  33.2 0.0 copy-start.4
  33.2 1.6 %scatter_own.1 = (f32[1,524288]{1,0:T(1,128)S(1)}, f32[1,128]{1,0:T(1,128)S(1)}, bf16[64,8192]{1,0:T(8,128)(2,1)}) custom-call(f32[32,1,2176]{2,1,0:T(1,128)S(1)} %all_to_all.5.got, f32[1,128]{1,0:T(1,128)S(1)} %rsqrt_minimum_fusion.factor, f32[64,8192]{1,0:T(8,128)S(1)} %get-tuple-element.37.rest_m, f32[64,8192]{1,0:T(8,128)S(1)} %get-tuple-element.38.rest_g), custom_call_target="tpu_custom_call" | custom-call | flops 300000000 | bytes 8388608 | tf_op jit(solution)/shard_map/scatter_own/pallas_call | solution.py:289
  34.8 0.0 collective-permute-done.2.got
  34.8 0.0 copy-done.1
  34.8 0.0 copy-done.4
  34.8 3.7 %merge_update.1 = (bf16[64,8192]{1,0:T(8,128)(2,1)}, bf16[64,256]{1,0:T(8,128)(2,1)}) custom-call(f32[32,1,2176]{2,1,0:T(1,128)S(1)} %collective-permute-done.2.got, f32[1,524288]{1,0:T(1,128)S(1)} %get-tuple-element.39.first, f32[1,128]{1,0:T(1,128)S(1)} %get-tuple-element.40.first_steps, ...), custom_call_target="tpu_custom_call", output_to_operand_aliasing={{1}: (7, {})} | custom-call | flops 1000000000 | bytes 2097152 | tf_op jit(solution)/shard_map/merge_update/pallas_call | solution.py:373
  (8 shorter events, 0.1 us)
Async XLA Ops:
  0.6 5.7 %copy-start.8 = (s32[1,16]{1,0:T(1,128)S(1)}, s32[1,16]{1,0:T(1,128)}, u32[]{:S(2)}) copy-start(s32[1,16]{1,0:T(1,128)} %param.18) | copy-start | bytes 196
  3.5 5.5 %collective-permute-start = (f32[1,128]{1,0:T(1,128)S(1)}, f32[1,128]{1,0:T(1,128)S(1)}, u32[]{:S(2)}, u32[]{:S(2)}) collective-permute-start(f32[1,128]{1,0:T(1,128)S(1)} %get-tuple-element.24), channel_id=1, source_target_pairs={{0,1},{1,0},{2,3},{3,2},{4,5},{5,4},{6,7},{7,6},{8,9},{9,8},{10,11... | collective-permute-start | bytes 1544 | tf_op jit(solution)/shard_map/ppermute | solution.py:416
  6.4 4.5 %copy-start = (bf16[1,64,8192]{2,1,0:T(8,128)(2,1)S(1)}, bf16[1,64,8192]{2,1,0:T(8,128)(2,1)}, u32[]{:S(2)}) copy-start(bf16[1,64,8192]{2,1,0:T(8,128)(2,1)} %param.17) | copy-start | bytes 3145732
  6.4 4.5 %copy-start.2 = (bf16[384,128]{1,0:T(8,128)(2,1)S(1)}, bf16[384,128]{1,0:T(8,128)(2,1)}, u32[]{:S(2)}) copy-start(bf16[384,128]{1,0:T(8,128)(2,1)} %constant.44.clone.back_right3) | copy-start | bytes 294916
  6.4 4.5 %copy-start.3 = (bf16[384,128]{1,0:T(8,128)(2,1)S(1)}, bf16[384,128]{1,0:T(8,128)(2,1)}, u32[]{:S(2)}) copy-start(bf16[384,128]{1,0:T(8,128)(2,1)} %constant.42.clone.right3) | copy-start | bytes 294916
  6.4 4.5 %copy-start.5 = (bf16[64,192]{1,0:T(8,128)(2,1)S(1)}, bf16[64,192]{1,0:T(8,128)(2,1)}, u32[]{:S(2)}) copy-start(bf16[64,192]{1,0:T(8,128)(2,1)} %constant.43.clone.back_left3) | copy-start | bytes 73732
  6.4 4.5 %copy-start.6 = (bf16[64,192]{1,0:T(8,128)(2,1)S(1)}, bf16[64,192]{1,0:T(8,128)(2,1)}, u32[]{:S(2)}) copy-start(bf16[64,192]{1,0:T(8,128)(2,1)} %constant.41.clone.left3) | copy-start | bytes 73732
  6.5 4.5 %copy-start.7 = (bf16[64,128]{1,0:T(8,128)(2,1)S(1)}, bf16[64,128]{1,0:T(8,128)(2,1)}, u32[]{:S(2)}) copy-start(bf16[64,128]{1,0:T(8,128)(2,1)} %constant.40.clone.left2) | copy-start | bytes 49156
  9.1 4.0 %collective-permute-start.1 = (f32[1,128]{1,0:T(1,128)S(1)}, f32[1,128]{1,0:T(1,128)S(1)}, u32[]{:S(2)}, u32[]{:S(2)}) collective-permute-start(f32[1,128]{1,0:T(1,128)S(1)} %add.21), channel_id=1, source_target_pairs={{0,3},{1,2},{2,1},{3,0},{4,7},{5,6},{6,5},{7,4},{8,11},{9,10},{10,... | collective-permute-start | bytes 1544 | tf_op jit(solution)/shard_map/ppermute | solution.py:419
  29.9 4.9 %collective-permute-start.2 = (f32[32,1,2176]{2,1,0:T(1,128)S(1)}, f32[32,1,2176]{2,1,0:T(1,128)S(1)}, u32[]{:S(2)}, u32[]{:S(2)}) collective-permute-start(f32[32,1,2176]{2,1,0:T(1,128)S(1)} %all_to_all.5.got), channel_id=1, source_target_pairs={{0,4},{4,0},{8,12},{12,8},{16,20},{20,16},{24,28},{28,24},{32,36},... | collective-permute-start | bytes 835592 | tf_op jit(solution)/shard_map/ppermute | solution.py:433
  33.2 1.6 %copy-start.1 = (bf16[256,256]{1,0:T(8,128)(2,1)S(1)}, bf16[256,256]{1,0:T(8,128)(2,1)}, u32[]{:S(2)}) copy-start(bf16[256,256]{1,0:T(8,128)(2,1)} %constant.46.clone.right2) | copy-start | bytes 393220
  33.2 1.6 %copy-start.4 = (bf16[64,192]{1,0:T(8,128)(2,1)S(1)}, bf16[64,192]{1,0:T(8,128)(2,1)}, u32[]{:S(2)}) copy-start(bf16[64,192]{1,0:T(8,128)(2,1)} %constant.45.clone.left3) | copy-start | bytes 73732

commit v8 on v7

--- a/solution.py
+++ b/solution.py
@@ -413,10 +413,10 @@
     grad, og_held, weight_held = [
         pltpu.with_memory_space_constraint(x, pltpu.VMEM) for x in (grad, og_held, weight_held)
     ]
-    squares = squares + lax.ppermute(squares, "shard", [(i, i ^ 1) for i in range(shards)])
+    squares = squares + lax.ppermute(squares, "shard", [(i, i ^ 3) for i in range(shards)])
     acts_grad = acts_grad_call(weight_held, og_held)
     squares, acts_grad = lax.optimization_barrier((squares, acts_grad))
-    squares = squares + lax.ppermute(squares, "shard", [(i, i ^ 3) for i in range(shards)])
+    squares = squares + lax.ppermute(squares, "shard", [(i, i ^ 1) for i in range(shards)])
     picks = chosen[0] % (rows * cols // 128)
     own_steps = steps.astype(F32)
     meta = jnp.concatenate([picks.astype(F32), own_steps, jnp.zeros((111,), F32)])

time: 38.6 us -> 38.3 us (level)
  starting transfers between devices: 7.32 us -> 6.9 us
    ppermute x1, starting transfers between devices: 2.13 us -> 0.09 us  [on_device(): lax.ppermute(squares, 'shard', [(i, i ^ 1) for i in range(shards)])]
    ppermute x1, starting transfers between devices: 1.9 us -> 3.39 us  [on_device(): lax.ppermute(squares, 'shard', [(i, i ^ 3) for i in range(shards)])]
  transfers between devices with their start and end apart: 3 -> 3, of which waited for: 0 -> 1; matrix products, arithmetic and copies ran while one was open for 0% -> 0% of each run, Pallas kernels for 14% -> 14%
where the time goes in v8:
time: 38.3 us; the launch traced here: 38.2 us
  blocking collectives  16.4 us (43%)
  Pallas kernels  12.1 us (32%)
  starting transfers between devices  6.9 us (18%)
  between operations  2.13 us (6%)
    all_to_all x1, blocking collectives, on_device(): lax.all_to_all(sent, 'island', 0, 0, tiled=True, axis_index_groups=same_c...  16.4 us
    pallas_call x1, Pallas kernels, merge_call(): pl.pallas_call(merge_kernel, in_specs=[vm] * 5 + [anyw] * 3, out_specs=[a...  3.67 us
    ppermute x1, starting transfers between devices, on_device(): swapped = lax.ppermute(got, 'island', other_core)  3.41 us
    ppermute x1, starting transfers between devices, on_device(): lax.ppermute(squares, 'shard', [(i, i ^ 3) for i in range(shards)])  3.39 us
    pallas_call x1, Pallas kernels, grad_call(): pl.pallas_call(grad_kernel, in_specs=[anyw] * 3, out_specs=[vm] * 4, out_...  2.89 us
    pallas_call x1, Pallas kernels, coef_call(): pl.pallas_call(coef_kernel, in_specs=[sm, sm] + [vm] * 7, out_specs=[vm]...  2.01 us
    pallas_call x1, Pallas kernels, acts_grad_call(): pl.pallas_call(acts_grad_kernel, in_specs=[vm, vm], out_specs=vm, out_sha...  1.91 us
    pallas_call x1, Pallas kernels, scatter_call(): pl.pallas_call(scatter_kernel, in_specs=[vm] * 4, out_specs=[vm, vm, pl.B...  1.58 us
  transfers between devices with their start and end apart: 3, of which 1 were waited for; matrix products, arithmetic and copies ran while one was open for 0% of the time, Pallas kernels for 14%

profile of v8, /device:TPU:1, one launch (start us, length us, event | category | flops | bytes accessed | tf_op | source)
XLA Modules:
  0.0 38.2 jit_solution(3162065619550706667)
XLA Ops:
  0.6 0.0 copy-start.8
  0.6 2.9 %weight_grad.1 = (f32[64,8192]{1,0:T(8,128)S(1)}, f32[1,128]{1,0:T(1,128)S(1)}, bf16[256,8192]{1,0:T(8,128)(2,1)S(1)}, bf16[64,8192]{1,0:T(8,128)(2,1)S(1)}) custom-call(bf16[64,256]{1,0:T(8,128)(2,1)} %acts.1, bf16[256,8192]{1,0:T(8,128)(2,1)} %og.3, bf16[64,8192]{1,0:T(8,128)(2,1)} %weight.3), custom_call_target="tpu_custom_call" | custom-call | flops 268435456 | bytes 6291456 | tf_op jit(solution)/shard_map/weight_grad/pallas_call | solution.py:99
  3.5 3.4 %collective-permute-start = (f32[1,128]{1,0:T(1,128)S(1)}, f32[1,128]{1,0:T(1,128)S(1)}, u32[]{:S(2)}, u32[]{:S(2)}) collective-permute-start(f32[1,128]{1,0:T(1,128)S(1)} %get-tuple-element.24), channel_id=1, source_target_pairs={{0,3},{1,2},{2,1},{3,0},{4,7},{5,6},{6,5},{7,4},{8,11},{9,10},{10,... | collective-permute-start | bytes 1544 | tf_op jit(solution)/shard_map/ppermute | solution.py:416
  7.6 0.0 copy-done.8
  7.6 0.1 pad_maximum_fusion
  7.7 0.0 copy-start
  7.7 0.0 copy-start.2
  7.7 0.0 copy-start.3
  7.7 0.0 copy-start.5
  7.7 0.0 copy-start.6
  7.7 0.0 copy-start.7
  7.7 1.9 %acts_grad.1.acts_early = bf16[64,256]{1,0:T(8,128)(2,1)} custom-call(bf16[64,8192]{1,0:T(8,128)(2,1)S(1)} %get-tuple-element.25.weight, bf16[256,8192]{1,0:T(8,128)(2,1)S(1)} %get-tuple-element.26.og), custom_call_target="tpu_custom_call" | custom-call | flops 268435456 | bytes 5242880 | tf_op jit(solution)/shard_map/acts_grad/pallas_call | solution.py:138
  10.3 0.0 collective-permute-done
  10.3 0.1 collective-permute-start.1
  10.4 0.0 copy-done
  10.4 0.0 copy-done.2
  10.4 0.0 copy-done.3
  10.5 0.0 copy-done.5
  10.5 0.0 copy-done.6
  10.5 0.0 copy-done.7
  10.5 2.0 %selected_coefs.1 = (f32[16,128]{1,0:T(8,128)S(1)}, f32[16,128]{1,0:T(8,128)S(1)}, f32[64,8192]{1,0:T(8,128)S(1)}, f32[64,8192]{1,0:T(8,128)S(1)}) custom-call(s32[16]{0:T(128)S(1)} %get-tuple-element.46.picks, s32[1]{0:T(128)} %bitcast.11.counts, bf16[64,8192]{1,0:T(8,128)(2,1)S(1)} %bitcast.12, f32[64,8192]{1,0:T(8,128)S(1)} %get-tuple-element.28.grad, ...), custom_call_target="tpu_custom_call" | custom-call | flops 300000000 | bytes 8388608 | tf_op jit(solution)/shard_map/selected_coefs/pallas_call | solution.py:205
  12.5 0.3 collective-permute-done.1
  12.9 0.1 broadcast_in_dim.21
  13.0 16.4 %all_to_all.5.got = f32[32,1,2176]{2,1,0:T(1,128)S(1)} all-to-all(f32[32,1,2176]{2,1,0:T(1,128)S(1)} %broadcast_in_dim.21), channel_id=1, replica_groups={{152,144,136,128,184,176,168,160,216,208,200,192,248,240,232,224,24,16,..., dimensions={0} | all-to-all | bytes 557056 | tf_op jit(solution)/shard_map/all_to_all | solution.py:432
  29.5 3.4 %collective-permute-start.2 = (f32[32,1,2176]{2,1,0:T(1,128)S(1)}, f32[32,1,2176]{2,1,0:T(1,128)S(1)}, u32[]{:S(2)}, u32[]{:S(2)}) collective-permute-start(f32[32,1,2176]{2,1,0:T(1,128)S(1)} %all_to_all.5.got), channel_id=1, source_target_pairs={{0,4},{4,0},{8,12},{12,8},{16,20},{20,16},{24,28},{28,24},{32,36},... | collective-permute-start | bytes 835592 | tf_op jit(solution)/shard_map/ppermute | solution.py:433
  32.9 0.0 copy-start.1
  32.9 0.0 copy-start.4
  32.9 1.6 %scatter_own.1 = (f32[1,524288]{1,0:T(1,128)S(1)}, f32[1,128]{1,0:T(1,128)S(1)}, bf16[64,8192]{1,0:T(8,128)(2,1)}) custom-call(f32[32,1,2176]{2,1,0:T(1,128)S(1)} %all_to_all.5.got, f32[1,128]{1,0:T(1,128)S(1)} %rsqrt_minimum_fusion.factor, f32[64,8192]{1,0:T(8,128)S(1)} %get-tuple-element.37.rest_m, f32[64,8192]{1,0:T(8,128)S(1)} %get-tuple-element.38.rest_g), custom_call_target="tpu_custom_call" | custom-call | flops 300000000 | bytes 8388608 | tf_op jit(solution)/shard_map/scatter_own/pallas_call | solution.py:289
  34.5 0.0 collective-permute-done.2.got
  34.5 0.0 copy-done.1
  34.5 0.0 copy-done.4
  34.5 3.7 %merge_update.1 = (bf16[64,8192]{1,0:T(8,128)(2,1)}, bf16[64,256]{1,0:T(8,128)(2,1)}) custom-call(f32[32,1,2176]{2,1,0:T(1,128)S(1)} %collective-permute-done.2.got, f32[1,524288]{1,0:T(1,128)S(1)} %get-tuple-element.39.first, f32[1,128]{1,0:T(1,128)S(1)} %get-tuple-element.40.first_steps, ...), custom_call_target="tpu_custom_call", output_to_operand_aliasing={{1}: (7, {})} | custom-call | flops 1000000000 | bytes 2097152 | tf_op jit(solution)/shard_map/merge_update/pallas_call | solution.py:373
  (8 shorter events, 0.1 us)
Async XLA Ops:
  0.6 7.0 %copy-start.8 = (s32[1,16]{1,0:T(1,128)S(1)}, s32[1,16]{1,0:T(1,128)}, u32[]{:S(2)}) copy-start(s32[1,16]{1,0:T(1,128)} %param.18) | copy-start | bytes 196
  3.5 6.8 %collective-permute-start = (f32[1,128]{1,0:T(1,128)S(1)}, f32[1,128]{1,0:T(1,128)S(1)}, u32[]{:S(2)}, u32[]{:S(2)}) collective-permute-start(f32[1,128]{1,0:T(1,128)S(1)} %get-tuple-element.24), channel_id=1, source_target_pairs={{0,3},{1,2},{2,1},{3,0},{4,7},{5,6},{6,5},{7,4},{8,11},{9,10},{10,... | collective-permute-start | bytes 1544 | tf_op jit(solution)/shard_map/ppermute | solution.py:416
  7.7 2.7 %copy-start = (bf16[1,64,8192]{2,1,0:T(8,128)(2,1)S(1)}, bf16[1,64,8192]{2,1,0:T(8,128)(2,1)}, u32[]{:S(2)}) copy-start(bf16[1,64,8192]{2,1,0:T(8,128)(2,1)} %param.17) | copy-start | bytes 3145732
  7.7 2.7 %copy-start.2 = (bf16[384,128]{1,0:T(8,128)(2,1)S(1)}, bf16[384,128]{1,0:T(8,128)(2,1)}, u32[]{:S(2)}) copy-start(bf16[384,128]{1,0:T(8,128)(2,1)} %constant.44.clone.back_right3) | copy-start | bytes 294916
  7.7 2.7 %copy-start.3 = (bf16[384,128]{1,0:T(8,128)(2,1)S(1)}, bf16[384,128]{1,0:T(8,128)(2,1)}, u32[]{:S(2)}) copy-start(bf16[384,128]{1,0:T(8,128)(2,1)} %constant.42.clone.right3) | copy-start | bytes 294916
  7.7 2.8 %copy-start.5 = (bf16[64,192]{1,0:T(8,128)(2,1)S(1)}, bf16[64,192]{1,0:T(8,128)(2,1)}, u32[]{:S(2)}) copy-start(bf16[64,192]{1,0:T(8,128)(2,1)} %constant.43.clone.back_left3) | copy-start | bytes 73732
  7.7 2.8 %copy-start.6 = (bf16[64,192]{1,0:T(8,128)(2,1)S(1)}, bf16[64,192]{1,0:T(8,128)(2,1)}, u32[]{:S(2)}) copy-start(bf16[64,192]{1,0:T(8,128)(2,1)} %constant.41.clone.left3) | copy-start | bytes 73732
  7.7 2.8 %copy-start.7 = (bf16[64,128]{1,0:T(8,128)(2,1)S(1)}, bf16[64,128]{1,0:T(8,128)(2,1)}, u32[]{:S(2)}) copy-start(bf16[64,128]{1,0:T(8,128)(2,1)} %constant.40.clone.left2) | copy-start | bytes 49156
  10.3 2.5 %collective-permute-start.1 = (f32[1,128]{1,0:T(1,128)S(1)}, f32[1,128]{1,0:T(1,128)S(1)}, u32[]{:S(2)}, u32[]{:S(2)}) collective-permute-start(f32[1,128]{1,0:T(1,128)S(1)} %add.21), channel_id=1, source_target_pairs={{0,1},{1,0},{2,3},{3,2},{4,5},{5,4},{6,7},{7,6},{8,9},{9,8},{10,11... | collective-permute-start | bytes 1544 | tf_op jit(solution)/shard_map/ppermute | solution.py:419
  29.5 5.0 %collective-permute-start.2 = (f32[32,1,2176]{2,1,0:T(1,128)S(1)}, f32[32,1,2176]{2,1,0:T(1,128)S(1)}, u32[]{:S(2)}, u32[]{:S(2)}) collective-permute-start(f32[32,1,2176]{2,1,0:T(1,128)S(1)} %all_to_all.5.got), channel_id=1, source_target_pairs={{0,4},{4,0},{8,12},{12,8},{16,20},{20,16},{24,28},{28,24},{32,36},... | collective-permute-start | bytes 835592 | tf_op jit(solution)/shard_map/ppermute | solution.py:433
  32.9 1.6 %copy-start.1 = (bf16[256,256]{1,0:T(8,128)(2,1)S(1)}, bf16[256,256]{1,0:T(8,128)(2,1)}, u32[]{:S(2)}) copy-start(bf16[256,256]{1,0:T(8,128)(2,1)} %constant.46.clone.right2) | copy-start | bytes 393220
  32.9 1.6 %copy-start.4 = (bf16[64,192]{1,0:T(8,128)(2,1)S(1)}, bf16[64,192]{1,0:T(8,128)(2,1)}, u32[]{:S(2)}) copy-start(bf16[64,192]{1,0:T(8,128)(2,1)} %constant.45.clone.left3) | copy-start | bytes 73732
